TPU v7x, 32 devices: a whole 2x2x4 slice. The times are simulated.
32 devices in a mesh: ctx: 4 (over x, core), fsdp: 8 (over z, y).
Axes of the slice: x: 2, y: 2, z: 4, core: 2. Of those that a mesh axis runs over, the one named last changes fastest.
Arguments:
- inputs: bfloat16 [8, 2048, 1024], P('fsdp', 'ctx'), may hold values from -6 to 6
- cotangent: bfloat16 [8, 2048, 1024], P('fsdp', 'ctx'), may hold values from -6 to 6
- block_table: int32 [8, 8], P('fsdp'), may hold values from 0 to 7, as said below
- attn_gain: bfloat16 [1024], P('fsdp'), may hold values from 0.5 to 1.5
- query_weight: bfloat16 [1024, 1024], P('fsdp'), may hold values from -0.1875 to 0.1875
- key_weight: bfloat16 [1024, 512], P('fsdp'), may hold values from -0.1875 to 0.1875
- value_weight: bfloat16 [1024, 512], P('fsdp'), may hold values from -0.1875 to 0.1875
- query_gain: bfloat16 [64], replicated, may hold values from 0.5 to 1.5
- key_gain: bfloat16 [64], replicated, may hold values from 0.5 to 1.5
- out_weight: bfloat16 [1024, 1024], P('fsdp'), may hold values from -2 to 2
- ffn_gain: bfloat16 [1024], P('fsdp'), may hold values from 0.5 to 1.5
- gate_weight: bfloat16 [1024, 4608], P('fsdp'), may hold values from -0.1875 to 0.1875
- up_weight: bfloat16 [1024, 4608], P('fsdp'), may hold values from -0.1875 to 0.1875
- down_weight: bfloat16 [4608, 1024], P('fsdp'), may hold values from -0.09375 to 0.09375
Outputs:
- output: bfloat16 [8, 2048, 1024], P('fsdp', 'ctx')
- input_grad: bfloat16 [8, 2048, 1024], P('fsdp', 'ctx')
- attn_gain_grad: float32 [1024], P('fsdp')
- query_weight_grad: float32 [1024, 1024], P('fsdp')
- key_weight_grad: float32 [1024, 512], P('fsdp')
- value_weight_grad: float32 [1024, 512], P('fsdp')
- query_gain_grad: float32 [64], replicated
- key_gain_grad: float32 [64], replicated
- out_weight_grad: float32 [1024, 1024], P('fsdp')
- ffn_gain_grad: float32 [1024], P('fsdp')
- gate_weight_grad: float32 [1024, 4608], P('fsdp')
- up_weight_grad: float32 [1024, 4608], P('fsdp')
- down_weight_grad: float32 [4608, 1024], P('fsdp')
Inputs may be any that keep to these rules, and one draw needn't show every extreme that they name: `block_table`: in every row, slots 2c and 2c + 1 hold blocks p and 7 - p, with p running over all of 0 to 3 once as c does; so every block appears once.
All inputs are finite; a program needn't handle non-finite values.
Results may differ from a plain program's by a relative error of at most 0.023.
Values may be sent and summed in bfloat16 or wider, within the bound.
A program may use at most 192 MiB of HBM per device.

v0:
```python
import jax
import jax.numpy as jnp
from jax import lax
from jax.sharding import PartitionSpec as P

epsilon = 1e-05
theta_base = 1000000.0


def rotary_tables(positions, width):
    half_width = width // 2
    freqs = theta_base ** (-jnp.arange(half_width, dtype=jnp.float32) * 2.0 / width)
    angles = positions.astype(jnp.float32)[:, None] * freqs[None, :]
    return (jnp.cos(angles)[:, None, :], jnp.sin(angles)[:, None, :])


def rotate(values, cosine, sine):
    half_width = values.shape[-1] // 2
    first_half = values[..., :half_width]
    second_half = values[..., half_width:]
    return jnp.concatenate(
        [first_half * cosine - second_half * sine, second_half * cosine + first_half * sine],
        axis=-1,
    )


def unrotate(grads, cosine, sine):
    half_width = grads.shape[-1] // 2
    first_half = grads[..., :half_width]
    second_half = grads[..., half_width:]
    return jnp.concatenate(
        [first_half * cosine + second_half * sine, second_half * cosine - first_half * sine],
        axis=-1,
    )


def head_norm(values, gain_vector):
    inverse = lax.rsqrt(jnp.mean(values * values, axis=-1, keepdims=True) + epsilon)
    unit_values = values * inverse
    return (unit_values * gain_vector, unit_values, inverse)


def norm_back(upstream, unit_values, inverse, gain_vector):
    scaled = upstream * gain_vector
    grad_in = inverse * (
        scaled - unit_values * jnp.mean(scaled * unit_values, axis=-1, keepdims=True)
    )
    return (grad_in, upstream * unit_values)


def outer_product(left, right):
    return lax.dot_general(
        left, right, (((0,), (0,)), ((), ())), preferred_element_type=jnp.float32
    )


def times_transposed(left, right):
    return lax.dot_general(
        left, right, (((1,), (1,)), ((), ())), preferred_element_type=jnp.float32
    )


def body(
    inputs,
    cotangent,
    block_table,
    attn_gain,
    query_weight,
    key_weight,
    value_weight,
    query_gain,
    key_gain,
    out_weight,
    ffn_gain,
    gate_weight,
    up_weight,
    down_weight,
):
    gain_attn_low, w_query, w_key, w_value, w_out, gain_ffn_low, w_gate, w_up, w_down = (
        lax.all_gather(attn_gain, "fsdp", axis=0, tiled=True),
        lax.all_gather(query_weight, "fsdp", axis=0, tiled=True),
        lax.all_gather(key_weight, "fsdp", axis=0, tiled=True),
        lax.all_gather(value_weight, "fsdp", axis=0, tiled=True),
        lax.all_gather(out_weight, "fsdp", axis=0, tiled=True),
        lax.all_gather(ffn_gain, "fsdp", axis=0, tiled=True),
        lax.all_gather(gate_weight, "fsdp", axis=0, tiled=True),
        lax.all_gather(up_weight, "fsdp", axis=0, tiled=True),
        lax.all_gather(down_weight, "fsdp", axis=0, tiled=True),
    )
    gain_attn = gain_attn_low.astype(jnp.float32)
    gain_ffn = gain_ffn_low.astype(jnp.float32)
    gain_query = query_gain.astype(jnp.float32)
    gain_key = key_gain.astype(jnp.float32)
    head_width = query_gain.shape[0]
    heads_count = w_query.shape[1] // head_width
    kv_count = w_key.shape[1] // head_width
    per_group = heads_count // kv_count
    group_width = per_group * head_width
    scale = head_width ** (-0.5)
    tokens = inputs.shape[1]
    half_block = tokens // 2
    table_row = block_table[0]
    block_count = table_row.shape[0]
    own_blocks = lax.dynamic_slice_in_dim(table_row, 2 * lax.axis_index("ctx"), 2)
    offsets = jnp.arange(half_block, dtype=jnp.int32)
    own_positions = (own_blocks[:, None] * half_block + offsets[None, :]).reshape(-1)
    all_positions = (table_row[:, None] * half_block + offsets[None, :]).reshape(-1)
    window_len = (block_count + 1) * half_block
    split_at = (block_count - own_blocks[0]) * half_block
    window_index = jnp.arange(window_len, dtype=jnp.int32)
    window_pos = jnp.where(window_index < split_at, window_index, window_index - split_at)
    slot_ids = jnp.arange(block_count, dtype=jnp.int32)
    slot_of_block = jnp.sum(
        jnp.where(table_row[None, :] == slot_ids[:, None], slot_ids[None, :], 0), axis=1
    )
    window_rows = (
        jnp.take(slot_of_block, window_pos // half_block) * half_block + window_pos % half_block
    )
    lower_query = jnp.arange(tokens, dtype=jnp.int32) < half_block
    second_part = window_index >= split_at
    visible = (own_positions[:, None] >= window_pos[None, :]) & (
        lower_query[:, None] == second_part[None, :]
    )
    hidden_in = inputs[0].astype(jnp.float32)
    inverse_one = lax.rsqrt(jnp.mean(hidden_in * hidden_in, axis=-1, keepdims=True) + epsilon)
    unit_one = hidden_in * inverse_one
    normed = (unit_one * gain_attn).astype(jnp.bfloat16)
    q_raw = jnp.dot(normed, w_query, preferred_element_type=jnp.float32)
    k_raw = jnp.dot(normed, w_key, preferred_element_type=jnp.float32)
    values_low = jnp.dot(normed, w_value, preferred_element_type=jnp.float32).astype(jnp.bfloat16)
    cosine, sine = rotary_tables(own_positions, head_width)
    q_normed, q_unit, q_inverse = head_norm(
        q_raw.reshape(tokens, heads_count, head_width), gain_query
    )
    k_normed, k_unit, k_inverse = head_norm(k_raw.reshape(tokens, kv_count, head_width), gain_key)
    queries = (
        rotate(q_normed, cosine, sine)
        .reshape(tokens, heads_count * head_width)
        .astype(jnp.bfloat16)
    )
    keys_low = (
        rotate(k_normed, cosine, sine).reshape(tokens, kv_count * head_width).astype(jnp.bfloat16)
    )
    key_all, value_all = (
        lax.all_gather(keys_low, "ctx", axis=0, tiled=True),
        lax.all_gather(values_low, "ctx", axis=0, tiled=True),
    )
    key_window = jnp.take(key_all, window_rows, axis=0)
    value_window = jnp.take(value_all, window_rows, axis=0)

    def scores_of(group):
        query_part = lax.dynamic_slice_in_dim(queries, group * group_width, group_width, 1).reshape(
            tokens, per_group, head_width
        )
        key_part = lax.dynamic_slice_in_dim(key_window, group * head_width, head_width, 1)
        value_part = lax.dynamic_slice_in_dim(value_window, group * head_width, head_width, 1)
        raw_scores = (
            jnp.einsum("thd,ld->htl", query_part, key_part, preferred_element_type=jnp.float32)
            * scale
        )
        return (jnp.where(visible[None], raw_scores, -1e30), query_part, key_part, value_part)

    def forward_group(group, carry):
        mixed_acc, logsum_acc = carry
        scores, query_part, key_part, value_part = scores_of(group)
        top_score = jnp.max(scores, axis=-1, keepdims=True)
        expo = jnp.exp(scores - top_score)
        total = jnp.sum(expo, axis=-1, keepdims=True)
        probs_low = (expo / total).astype(jnp.bfloat16)
        attended = jnp.einsum(
            "htl,ld->thd", probs_low, value_part, preferred_element_type=jnp.float32
        )
        mixed_acc = lax.dynamic_update_slice_in_dim(
            mixed_acc,
            attended.reshape(tokens, group_width).astype(jnp.bfloat16),
            group * group_width,
            1,
        )
        logsum_acc = lax.dynamic_update_slice_in_dim(
            logsum_acc, (top_score + jnp.log(total))[..., 0], group * per_group, 0
        )
        return (mixed_acc, logsum_acc)

    mixed, logsum = lax.fori_loop(
        0,
        kv_count,
        forward_group,
        (
            jnp.zeros((tokens, heads_count * head_width), jnp.bfloat16),
            jnp.zeros((heads_count, tokens), jnp.float32),
        ),
    )
    resid = hidden_in + jnp.dot(mixed, w_out, preferred_element_type=jnp.float32)
    inverse_two = lax.rsqrt(jnp.mean(resid * resid, axis=-1, keepdims=True) + epsilon)
    unit_two = resid * inverse_two
    ffn_in = (unit_two * gain_ffn).astype(jnp.bfloat16)
    gate = jnp.dot(ffn_in, w_gate, preferred_element_type=jnp.float32)
    up_part = jnp.dot(ffn_in, w_up, preferred_element_type=jnp.float32)
    sigma = jax.nn.sigmoid(gate)
    silu_gate = gate * sigma
    hidden = (silu_gate * up_part).astype(jnp.bfloat16)
    output = (resid + jnp.dot(hidden, w_down, preferred_element_type=jnp.float32)).astype(
        jnp.bfloat16
    )
    grad_out = cotangent[0]
    down_grad = outer_product(hidden, grad_out)
    grad_hidden = times_transposed(grad_out, w_down)
    grad_gate = (grad_hidden * up_part * sigma * (1.0 + gate * (1.0 - sigma))).astype(jnp.bfloat16)
    grad_up = (grad_hidden * silu_gate).astype(jnp.bfloat16)
    gate_grad = outer_product(ffn_in, grad_gate)
    up_grad = outer_product(ffn_in, grad_up)
    grad_ffn_in = times_transposed(grad_gate, w_gate) + times_transposed(grad_up, w_up)
    grad_resid_norm, ffn_gain_terms = norm_back(grad_ffn_in, unit_two, inverse_two, gain_ffn)
    ffn_gain_sum = jnp.sum(ffn_gain_terms, axis=0)
    grad_resid = grad_out.astype(jnp.float32) + grad_resid_norm
    grad_attn = grad_resid.astype(jnp.bfloat16)
    out_grad = outer_product(mixed, grad_attn)
    grad_mixed = times_transposed(grad_attn, w_out).astype(jnp.bfloat16)

    def backward_group(group, carry):
        grad_queries, grad_keys, grad_values = carry
        scores, query_part, key_part, value_part = scores_of(group)
        logsum_part = lax.dynamic_slice_in_dim(logsum, group * per_group, per_group, 0)
        probs = jnp.exp(scores - logsum_part[:, :, None])
        upstream = lax.dynamic_slice_in_dim(
            grad_mixed, group * group_width, group_width, 1
        ).reshape(tokens, per_group, head_width)
        grad_probs = jnp.einsum(
            "thd,ld->htl", upstream, value_part, preferred_element_type=jnp.float32
        )
        delta = jnp.sum(probs * grad_probs, axis=-1, keepdims=True)
        grad_scores = (probs * (grad_probs - delta)).astype(jnp.bfloat16)
        query_term = (
            jnp.einsum("htl,ld->thd", grad_scores, key_part, preferred_element_type=jnp.float32)
            * scale
        )
        key_term = (
            jnp.einsum("htl,thd->ld", grad_scores, query_part, preferred_element_type=jnp.float32)
            * scale
        )
        value_term = jnp.einsum(
            "htl,thd->ld", probs.astype(jnp.bfloat16), upstream, preferred_element_type=jnp.float32
        )
        grad_queries = lax.dynamic_update_slice_in_dim(
            grad_queries, query_term.reshape(tokens, group_width), group * group_width, 1
        )
        grad_keys = lax.dynamic_update_slice_in_dim(grad_keys, key_term, group * head_width, 1)
        grad_values = lax.dynamic_update_slice_in_dim(
            grad_values, value_term, group * head_width, 1
        )
        return (grad_queries, grad_keys, grad_values)

    grad_queries, grad_keys_window, grad_values_window = lax.fori_loop(
        0,
        kv_count,
        backward_group,
        (
            jnp.zeros((tokens, heads_count * head_width), jnp.float32),
            jnp.zeros((window_len, kv_count * head_width), jnp.float32),
            jnp.zeros((window_len, kv_count * head_width), jnp.float32),
        ),
    )
    first_valid = (all_positions < split_at)[:, None]
    second_index = jnp.minimum(all_positions + split_at, window_len - 1)
    second_valid = (all_positions + split_at < window_len)[:, None]
    first_index = jnp.minimum(all_positions, window_len - 1)

    def back_to_rows(window_grad):
        return jnp.where(first_valid, jnp.take(window_grad, first_index, axis=0), 0.0) + jnp.where(
            second_valid, jnp.take(window_grad, second_index, axis=0), 0.0
        )

    grad_keys_all = back_to_rows(grad_keys_window)
    grad_values_all = back_to_rows(grad_values_window)
    grad_keys_own, grad_values_own = (
        lax.psum_scatter(
            grad_keys_all.astype(jnp.bfloat16), "ctx", scatter_dimension=0, tiled=True
        ).astype(jnp.float32),
        lax.psum_scatter(
            grad_values_all.astype(jnp.bfloat16), "ctx", scatter_dimension=0, tiled=True
        ).astype(jnp.float32),
    )
    grad_q_normed = unrotate(grad_queries.reshape(tokens, heads_count, head_width), cosine, sine)
    grad_q_raw, query_gain_terms = norm_back(grad_q_normed, q_unit, q_inverse, gain_query)
    grad_k_normed = unrotate(grad_keys_own.reshape(tokens, kv_count, head_width), cosine, sine)
    grad_k_raw, key_gain_terms = norm_back(grad_k_normed, k_unit, k_inverse, gain_key)
    grad_q_low = grad_q_raw.reshape(tokens, heads_count * head_width).astype(jnp.bfloat16)
    grad_k_low = grad_k_raw.reshape(tokens, kv_count * head_width).astype(jnp.bfloat16)
    grad_v_low = grad_values_own.astype(jnp.bfloat16)
    query_grad = outer_product(normed, grad_q_low)
    key_grad = outer_product(normed, grad_k_low)
    value_grad = outer_product(normed, grad_v_low)
    grad_normed = (
        times_transposed(grad_q_low, w_query)
        + times_transposed(grad_k_low, w_key)
        + times_transposed(grad_v_low, w_value)
    )
    grad_input_norm, attn_gain_terms = norm_back(grad_normed, unit_one, inverse_one, gain_attn)
    input_grad = (grad_resid + grad_input_norm).astype(jnp.bfloat16)
    attn_gain_sum = jnp.sum(attn_gain_terms, axis=0)
    pieces = (
        lax.psum_scatter(
            attn_gain_sum.astype(jnp.bfloat16), "fsdp", scatter_dimension=0, tiled=True
        ).astype(jnp.float32),
        lax.psum_scatter(
            query_grad.astype(jnp.bfloat16), "fsdp", scatter_dimension=0, tiled=True
        ).astype(jnp.float32),
        lax.psum_scatter(
            key_grad.astype(jnp.bfloat16), "fsdp", scatter_dimension=0, tiled=True
        ).astype(jnp.float32),
        lax.psum_scatter(
            value_grad.astype(jnp.bfloat16), "fsdp", scatter_dimension=0, tiled=True
        ).astype(jnp.float32),
        lax.psum_scatter(
            out_grad.astype(jnp.bfloat16), "fsdp", scatter_dimension=0, tiled=True
        ).astype(jnp.float32),
        lax.psum_scatter(
            ffn_gain_sum.astype(jnp.bfloat16), "fsdp", scatter_dimension=0, tiled=True
        ).astype(jnp.float32),
        lax.psum_scatter(
            gate_grad.astype(jnp.bfloat16), "fsdp", scatter_dimension=0, tiled=True
        ).astype(jnp.float32),
        lax.psum_scatter(
            up_grad.astype(jnp.bfloat16), "fsdp", scatter_dimension=0, tiled=True
        ).astype(jnp.float32),
        lax.psum_scatter(
            down_grad.astype(jnp.bfloat16), "fsdp", scatter_dimension=0, tiled=True
        ).astype(jnp.float32),
    )
    owned = (
        lax.psum(pieces[0].astype(jnp.bfloat16), "ctx").astype(jnp.float32),
        lax.psum(pieces[1].astype(jnp.bfloat16), "ctx").astype(jnp.float32),
        lax.psum(pieces[2].astype(jnp.bfloat16), "ctx").astype(jnp.float32),
        lax.psum(pieces[3].astype(jnp.bfloat16), "ctx").astype(jnp.float32),
        lax.psum(pieces[4].astype(jnp.bfloat16), "ctx").astype(jnp.float32),
        lax.psum(pieces[5].astype(jnp.bfloat16), "ctx").astype(jnp.float32),
        lax.psum(pieces[6].astype(jnp.bfloat16), "ctx").astype(jnp.float32),
        lax.psum(pieces[7].astype(jnp.bfloat16), "ctx").astype(jnp.float32),
        lax.psum(pieces[8].astype(jnp.bfloat16), "ctx").astype(jnp.float32),
    )
    query_gain_grad, key_gain_grad = lax.psum(
        (jnp.sum(query_gain_terms, axis=(0, 1)), jnp.sum(key_gain_terms, axis=(0, 1))),
        ("ctx", "fsdp"),
    )
    return (
        output[None],
        input_grad[None],
        owned[0],
        owned[1],
        owned[2],
        owned[3],
        query_gain_grad,
        key_gain_grad,
        owned[4],
        owned[5],
        owned[6],
        owned[7],
        owned[8],
    )


def solution(mesh):
    return jax.shard_map(
        body,
        mesh=mesh,
        in_specs=(
            P("fsdp", "ctx", None),
            P("fsdp", "ctx", None),
            P("fsdp", None),
            P("fsdp"),
            P("fsdp", None),
            P("fsdp", None),
            P("fsdp", None),
            P(),
            P(),
            P("fsdp", None),
            P("fsdp"),
            P("fsdp", None),
            P("fsdp", None),
            P("fsdp", None),
        ),
        out_specs=(
            P("fsdp", "ctx", None),
            P("fsdp", "ctx", None),
            P("fsdp"),
            P("fsdp", None),
            P("fsdp", None),
            P("fsdp", None),
            P(),
            P(),
            P("fsdp", None),
            P("fsdp"),
            P("fsdp", None),
            P("fsdp", None),
            P("fsdp", None),
        ),
        check_vma=False,
    )
```

profile of v0, /device:TPU:0, one launch (start us, length us, event | category | flops | bytes accessed | tf_op | source)
XLA Modules:
  0.0 2049.1 jit_solution(690131233395850377)
XLA Ops:
  9.5 22.3 %all-gather = bf16[8,1,128]{2,1,0:T(2,128)(2,1)S(1)} all-gather(bf16[1,1,128]{2,1,0:T(2,128)(2,1)} %bitcast.285), channel_id=1, replica_groups=mesh['ctx'=4,'fsdp'=8] {'fsdp'}, dimensions={0}, use_global_device_ids=true | all-gather | bytes 2304 | tf_op jit(solution)/shard_map/all_gather | solution.py:80
  35.2 17.9 all-gather.16.cloned.1.call-done
  57.5 36.7 %all-gather.12.cloned.1.call-done = bf16[1024,512]{1,0:T(8,128)(2,1)} async-done(((bf16[128,512]{1,0:T(8,128)(2,1)}), bf16[1024,512]{1,0:T(8,128)(2,1)}) %all-gather.12.cloned.1.call-update) | async-done | bytes 1048592 | tf_op jit(solution)/shard_map/all_gather | solution.py:83
  108.2 18.3 all-gather.1
  127.7 16.6 all-gather.20.cloned.1.call-done
  151.1 16.4 all-gather.18.cloned.1.call-done
  167.5 9.5 gather_fusion.1
  176.9 15.1 all-gather.14.cloned.1.call-done
  192.1 9.5 gather_fusion
  215.6 154.3 %while.34 = (s32[]{:T(128)}, bf16[512,1024]{0,1:T(8,128)(2,1)}, f32[16,512]{1,0:T(8,128)S(1)}, bf16[2304,512]{0,1:T(8,128)(2,1)}, bf16[2304,512]{0,1:T(8,128)(2,...) while((s32[]{:T(128)}, bf16[512,1024]{0,1:T(8,128)(2,1)}, ...), condition=%wide.region_7.9_spmd.clone, body=%wide.region_4.8_spmd.clone.sunk | while | flops 635894784 | bytes 72202328 | solution.py:184
  227.6 6.8 fusion.160
  246.8 6.7 fusion.160
  266.0 6.8 fusion.160
  285.2 6.7 fusion.160
  305.0 6.8 fusion.160
  324.2 6.7 fusion.160
  343.4 6.7 fusion.160
  373.5 8.6 all-gather.24.cloned.1.call-done
  382.1 11.2 fusion.93
  393.3 127.3 %all-gather.26.cloned.1.call-done = bf16[1024,4608]{1,0:T(8,128)(2,1)} async-done(((bf16[128,4608]{1,0:T(8,128)(2,1)}), bf16[1024,4608]{1,0:T(8,128)(2,1)}) %all-gather.26.cloned.1.call-update) | async-done | bytes 9437200 | tf_op jit(solution)/shard_map/all_gather | solution.py:87
  520.6 11.5 fusion.94
  532.1 126.9 %all-gather.28.cloned.1.call-done = bf16[4608,1024]{1,0:T(8,128)(2,1)} async-done(((bf16[576,1024]{1,0:T(8,128)(2,1)}), bf16[4608,1024]{1,0:T(8,128)(2,1)}) %all-gather.28.cloned.1.call-update) | async-done | bytes 9437200 | tf_op jit(solution)/shard_map/all_gather | solution.py:88
  659.1 18.0 multiply_convert_fusion
  677.1 9.2 fusion.95
  686.3 8.7 multiply_reduce_fusion
  704.1 330.8 %while.35 = (s32[]{:T(128)}, f32[512,1024]{0,1:T(8,128)S(1)}, f32[2304,512]{0,1:T(8,128)}, f32[2304,512]{0,1:T(8,128)}, bf16[2304,512]{0,1:T(8,128)(2,1)}, /*ind...) while((s32[]{:T(128)}, f32[512,1024]{0,1:T(8,128)S(1)}, ...), condition=%wide.region_12.14_spmd.clone, body=%wide.region_10.13_spmd.clone.sunk | while | flops 1534934016 | bytes 96209024 | solution.py:253
  714.2 7.5 fusion.171
  721.7 11.0 fusion.172
  755.5 7.5 fusion.171
  763.0 11.0 fusion.172
  796.9 7.5 fusion.171
  804.4 11.0 fusion.172
  838.2 7.5 fusion.171
  845.7 11.0 fusion.172
  879.5 7.5 fusion.171
  887.0 11.0 fusion.172
  920.8 7.5 fusion.171
  928.3 11.0 fusion.172
  962.1 7.5 fusion.171
  969.7 11.0 fusion.172
  1003.5 7.5 fusion.171
  1011.0 11.0 fusion.172
  1034.9 6.8 copy.93
  1047.7 11.8 gather_fusion.4
  1059.6 11.9 gather_fusion.2
  1071.5 11.9 gather_fusion.3
  1083.4 11.8 gather_fusion.5
  1095.2 8.6 fusion.44
  1116.3 17.3 reduce-scatter.10.cloned.1.call-done
  1140.7 27.6 %reduce-scatter.12.cloned.1.call-done = bf16[512,512]{1,0:T(8,128)(2,1)} async-done(((bf16[2048,512]{1,0:T(8,128)(2,1)}), bf16[512,512]{1,0:T(8,128)(2,1)}) %reduce-scatter.12.cloned.1.call-update) | async-done | bytes 524304 | tf_op jit(solution)/shard_map/reduce_scatter | solution.py:279
  1171.2 9.8 convolution_convert_fusion.2
  1181.1 9.8 convolution_convert_fusion.1
  1192.2 10.1 convolution_convert_fusion
  1204.2 35.4 %reduce-scatter.14.cloned.1.call-done = bf16[128,1024]{1,0:T(8,128)(2,1)} async-done(((bf16[1024,1024]{1,0:T(8,128)(2,1)}), bf16[128,1024]{1,0:T(8,128)(2,1)}) %reduce-scatter.14.cloned.1.call-update) | async-done | bytes 262160 | tf_op jit(solution)/shard_map/reduce_scatter | solution.py:305
  1239.6 70.3 %reduce-scatter.20.cloned.1.call-done = bf16[128,1024]{1,0:T(8,128)(2,1)} async-done(((bf16[1024,1024]{1,0:T(8,128)(2,1)}), bf16[128,1024]{1,0:T(8,128)(2,1)}) %reduce-scatter.20.cloned.1.call-update) | async-done | bytes 262160 | tf_op jit(solution)/shard_map/reduce_scatter | solution.py:314
  1309.8 66.2 %reduce-scatter.16.cloned.1.call-done = bf16[128,512]{1,0:T(8,128)(2,1)} async-done(((bf16[1024,512]{1,0:T(8,128)(2,1)}), bf16[128,512]{1,0:T(8,128)(2,1)}) %reduce-scatter.16.cloned.1.call-update) | async-done | bytes 131088 | tf_op jit(solution)/shard_map/reduce_scatter | solution.py:308
  1376.1 66.7 %reduce-scatter.18.cloned.1.call-done = bf16[128,512]{1,0:T(8,128)(2,1)} async-done(((bf16[1024,512]{1,0:T(8,128)(2,1)}), bf16[128,512]{1,0:T(8,128)(2,1)}) %reduce-scatter.18.cloned.1.call-update) | async-done | bytes 131088 | tf_op jit(solution)/shard_map/reduce_scatter | solution.py:311
  1442.8 166.0 %reduce-scatter.22.cloned.1.call-done = bf16[128,4608]{1,0:T(8,128)(2,1)} async-done(((bf16[1024,4608]{1,0:T(8,128)(2,1)}), bf16[128,4608]{1,0:T(8,128)(2,1)}) %reduce-scatter.22.cloned.1.call-update) | async-done | bytes 1179664 | tf_op jit(solution)/shard_map/reduce_scatter | solution.py:320
  1608.7 166.0 %reduce-scatter.24.cloned.1.call-done = bf16[128,4608]{1,0:T(8,128)(2,1)} async-done(((bf16[1024,4608]{1,0:T(8,128)(2,1)}), bf16[128,4608]{1,0:T(8,128)(2,1)}) %reduce-scatter.24.cloned.1.call-update) | async-done | bytes 1179664 | tf_op jit(solution)/shard_map/reduce_scatter | solution.py:323
  1774.7 166.0 %reduce-scatter.26.cloned.1.call-done = bf16[576,1024]{1,0:T(8,128)(2,1)} async-done(((bf16[4608,1024]{1,0:T(8,128)(2,1)}), bf16[576,1024]{1,0:T(8,128)(2,1)}) %reduce-scatter.26.cloned.1.call-update) | async-done | bytes 1179664 | tf_op jit(solution)/shard_map/reduce_scatter | solution.py:326
  1940.8 9.9 fusion.64
  1955.8 19.6 all-reduce.3
  1983.1 37.2 %all-reduce.2 = (f32[64]{0:T(128)}, f32[64]{0:T(128)}) all-reduce(f32[64]{0:T(128)S(1)} %get-tuple-element.466, f32[64]{0:T(128)S(1)} %get-tuple-element.472), channel_id=1, replica_groups=mesh['ctx'=4,'fsdp'=8] {'ctx','fsdp'}, use_global_device_ids=true, to_apply=%region_28.31 | all-reduce | flops 128 | bytes 1024 | tf_op jit(solution)/shard_map/psum | solution.py:341
  2023.5 9.1 all-reduce.8.cloned.1.call-done
  (409 shorter events, 402.6 us)
Async XLA Ops:
  7.2 47.4 %copy-start.6 = (bf16[1,512,1024]{2,1,0:T(8,128)(2,1)S(1)}, bf16[1,512,1024]{2,1,0:T(8,128)(2,1)}, u32[]{:S(2)}) copy-start(bf16[1,512,1024]{2,1,0:T(8,128)(2,1)} %param.22) | copy-start | bytes 3145732
  7.2 45.9 %all-gather.16.cloned.1.call-start = ((), (), s32[]{:S(2)}) async-start(), calls=%async_computation.11 | async-start | bytes 1179648 | tf_op jit(solution)/shard_map/all_gather | solution.py:82
  7.9 86.2 %all-gather.12.cloned.1.call-start = ((), (), s32[]{:S(2)}) async-start(), calls=%async_computation.9 | async-start | bytes 1179648 | tf_op jit(solution)/shard_map/all_gather | solution.py:83
  8.7 135.7 %all-gather.20.cloned.1.call-start = ((), (), s32[]{:S(2)}) async-start(), calls=%async_computation.13 | async-start | bytes 2359296 | tf_op jit(solution)/shard_map/all_gather | solution.py:81
  9.4 158.0 %all-gather.18.cloned.1.call-start = ((), (), s32[]{:S(2)}) async-start(), calls=%async_computation.12 | async-start | bytes 2621440 | tf_op jit(solution)/shard_map/all_gather | solution.py:145
  31.8 115.4 %copy-start.43 = (f32[8,1,128]{2,1,0:T(1,128)}, f32[8,1,128]{2,1,0:T(1,128)S(1)}, u32[]{:S(2)}) copy-start(f32[8,1,128]{2,1,0:T(1,128)S(1)} %convert_element_type.257) | copy-start | bytes 12292
  32.5 23.0 %copy-start.53 = (f32[64]{0:T(128)}, f32[64]{0:T(128)S(1)}, u32[]{:S(2)}) copy-start(f32[64]{0:T(128)S(1)} %convert_element_type.217) | copy-start | bytes 772
  34.8 112.4 %copy-start.45 = (f32[512]{0:T(512)}, f32[512]{0:T(512)S(1)}, u32[]{:S(2)}) copy-start(f32[512]{0:T(512)S(1)} %add_rsqrt_fusion.3) | copy-start | bytes 6148
  35.1 114.0 %copy-start.19 = (f32[512,32]{0,1:T(8,128)}, f32[512,32]{0,1:T(8,128)S(1)}, u32[]{:S(2)}) copy-start(f32[512,32]{0,1:T(8,128)S(1)} %get-tuple-element.556) | copy-start | bytes 196612
  35.1 114.0 %copy-start.21 = (f32[512,32]{0,1:T(8,128)}, f32[512,32]{0,1:T(8,128)S(1)}, u32[]{:S(2)}) copy-start(f32[512,32]{0,1:T(8,128)S(1)} %get-tuple-element.557) | copy-start | bytes 196612
  57.4 134.6 %all-gather.14.cloned.1.call-start = ((), (), s32[]{:S(2)}) async-start(), calls=%async_computation.10 | async-start | bytes 2621440 | tf_op jit(solution)/shard_map/all_gather | solution.py:146
  96.9 11.2 copy-start.58
  96.9 11.3 copy-start.56
  97.0 273.0 %all-gather.22.cloned.1.call-start = ((), (), s32[]{:S(2)}) async-start(), calls=%async_computation.14 | async-start | bytes 2359296 | tf_op jit(solution)/shard_map/all_gather | solution.py:84
  97.5 284.6 %all-gather.24.cloned.1.call-start = ((), (), s32[]{:S(2)}) async-start(), calls=%async_computation.15 | async-start | bytes 10616832 | tf_op jit(solution)/shard_map/all_gather | solution.py:86
  98.3 422.3 %all-gather.26.cloned.1.call-start = ((), (), s32[]{:S(2)}) async-start(), calls=%async_computation.16 | async-start | bytes 10616832 | tf_op jit(solution)/shard_map/all_gather | solution.py:87
  99.0 560.0 %all-gather.28.cloned.1.call-start = ((), (), s32[]{:S(2)}) async-start(), calls=%async_computation.17 | async-start | bytes 10616832 | tf_op jit(solution)/shard_map/all_gather | solution.py:88
  99.8 1033.8 %reduce-scatter.10.cloned.1.call-start = ((), (), s32[]{:S(2)}) async-start(), calls=%async_computation.18 | async-start | bytes 2621440 | tf_op jit(solution)/shard_map/reduce_scatter | solution.py:276
  108.2 40.5 %copy-start.51 = (f32[64]{0:T(128)}, f32[64]{0:T(128)S(1)}, u32[]{:S(2)}) copy-start(f32[64]{0:T(128)S(1)} %convert_element_type.220) | copy-start | bytes 772
  221.6 3.7 copy-start.1
  240.8 3.7 copy-start.1
  260.0 3.7 copy-start.1
  279.2 3.7 copy-start.1
  298.4 4.3 copy-start.1
  318.2 3.7 copy-start.1
  337.4 3.7 copy-start.1
  356.6 3.7 copy-start.1
  373.3 321.7 %copy-start.4 = (f32[512,1024]{1,0:T(8,128)}, f32[512,1024]{1,0:T(8,128)S(1)}, u32[]{:S(2)}) copy-start(f32[512,1024]{1,0:T(8,128)S(1)} %get-tuple-element.575) | copy-start | bytes 6291460
  373.5 147.1 %copy-start.25 = (bf16[512,1024]{1,0:T(8,128)(2,1)}, bf16[512,1024]{1,0:T(8,128)(2,1)S(1)}, u32[]{:S(2)}) copy-start(bf16[512,1024]{1,0:T(8,128)(2,1)S(1)} %multiply_convert_fusion.4) | copy-start | bytes 3145732
  677.1 9.2 copy-start.60
  686.3 8.7 copy-start.27
  732.8 4.9 copy-start
  774.1 4.9 copy-start
  815.5 4.8 copy-start
  856.8 4.8 copy-start
  898.0 4.8 copy-start
  939.3 4.9 copy-start
  980.7 4.9 copy-start
  1022.0 4.9 copy-start
  1034.9 6.8 copy-start.10
  1041.7 6.0 copy-start.41
  1059.6 11.9 copy-start.42
  1083.3 11.8 copy-start.47
  1083.3 11.8 copy-start.48
  1083.3 11.8 copy-start.49
  1083.3 11.8 copy-start.50
  1103.8 64.5 %reduce-scatter.12.cloned.1.call-start = ((), (), s32[]{:S(2)}) async-start(), calls=%async_computation.19 | async-start | bytes 2621440 | tf_op jit(solution)/shard_map/reduce_scatter | solution.py:279
  1104.6 135.0 %reduce-scatter.14.cloned.1.call-start = ((), (), s32[]{:S(2)}) async-start(), calls=%async_computation.20 | async-start | bytes 2359296 | tf_op jit(solution)/shard_map/reduce_scatter | solution.py:305
  1112.3 197.5 %reduce-scatter.20.cloned.1.call-start = ((), (), s32[]{:S(2)}) async-start(), calls=%async_computation.23 | async-start | bytes 2359296 | tf_op jit(solution)/shard_map/reduce_scatter | solution.py:314
  1116.2 21.0 %copy-start.9 = (f32[512,8,64]{0,2,1:T(8,128)S(1)}, f32[512,8,64]{0,2,1:T(8,128)}, u32[]{:S(2)}) copy-start(f32[512,8,64]{0,2,1:T(8,128)} %copy-done.8) | copy-start | bytes 3145732
  1116.2 21.0 %copy-start.36 = (f32[512,8]{0,1:T(8,128)S(1)}, f32[512,8]{0,1:T(8,128)}, u32[]{:S(2)}) copy-start(f32[512,8]{0,1:T(8,128)} %copy-done.35) | copy-start | bytes 49156
  1116.2 21.0 %copy-start.54 = (f32[64]{0:T(128)S(1)}, f32[64]{0:T(128)}, u32[]{:S(2)}) copy-start(f32[64]{0:T(128)} %copy-done.53) | copy-start | bytes 772
  1116.2 259.8 %reduce-scatter.16.cloned.1.call-start = ((), (), s32[]{:S(2)}) async-start(), calls=%async_computation.21 | async-start | bytes 1179648 | tf_op jit(solution)/shard_map/reduce_scatter | solution.py:308
  1140.6 30.6 %copy-start.26 = (bf16[512,1024]{1,0:T(8,128)(2,1)S(1)}, bf16[512,1024]{1,0:T(8,128)(2,1)}, u32[]{:S(2)}) copy-start(bf16[512,1024]{1,0:T(8,128)(2,1)} %copy-done.25) | copy-start | bytes 3145732
  1140.6 302.2 %reduce-scatter.18.cloned.1.call-start = ((), (), s32[]{:S(2)}) async-start(), calls=%async_computation.22 | async-start | bytes 1179648 | tf_op jit(solution)/shard_map/reduce_scatter | solution.py:311
  1171.2 437.5 %reduce-scatter.22.cloned.1.call-start = ((), (), s32[]{:S(2)}) async-start(), calls=%async_computation.24 | async-start | bytes 10616832 | tf_op jit(solution)/shard_map/reduce_scatter | solution.py:320
  1181.1 593.7 %reduce-scatter.24.cloned.1.call-start = ((), (), s32[]{:S(2)}) async-start(), calls=%async_computation.25 | async-start | bytes 10616832 | tf_op jit(solution)/shard_map/reduce_scatter | solution.py:323
  1191.0 749.8 %reduce-scatter.26.cloned.1.call-start = ((), (), s32[]{:S(2)}) async-start(), calls=%async_computation.26 | async-start | bytes 10616832 | tf_op jit(solution)/shard_map/reduce_scatter | solution.py:326
  1202.3 738.5 %copy-start.5 = (f32[512,1024]{1,0:T(8,128)S(1)}, f32[512,1024]{1,0:T(8,128)}, u32[]{:S(2)}) copy-start(f32[512,1024]{1,0:T(8,128)} %copy-done.4) | copy-start | bytes 6291460
  1202.3 830.3 %all-reduce.8.cloned.1.call-start = ((), (), s32[]{:S(2)}) async-start(), calls=%async_computation.27 | async-start | bytes 8650752 | tf_op jit(solution)/shard_map/psum | solution.py:332
  1940.8 9.9 copy-start.15
  1940.8 9.9 copy-start.30
  1953.4 66.9 %copy-start.13 = (f32[512,1024]{1,0:T(8,128)S(1)}, f32[512,1024]{1,0:T(8,128)}, u32[]{:S(2)}) copy-start(f32[512,1024]{1,0:T(8,128)} %copy-done.11) | copy-start | bytes 6291460
  2037.2 4.1 copy-start.39
  (30 other events, 52.4 us)
Sparse Core Ops, SparseCore 0:
  10.1 42.8 all-gather.15
  55.2 38.8 all-gather.11
  96.3 48.0 all-gather.19
  146.3 21.0 all-gather.17
  169.4 22.5 all-gather.13
  194.0 49.2 all-gather.21
  245.6 136.5 all-gather.23
  384.3 136.2 all-gather.25
  522.8 136.2 all-gather.27
  1103.9 29.5 reduce-scatter.9
  1136.8 31.4 reduce-scatter.11
  1171.7 67.8 reduce-scatter.13
  1243.1 66.6 reduce-scatter.19
  1313.7 62.3 reduce-scatter.15
  1380.3 62.4 reduce-scatter.17
  1446.2 162.4 reduce-scatter.21
  1612.2 162.5 reduce-scatter.23
  1778.2 162.5 reduce-scatter.25
  1943.6 88.9 all-reduce.7
where the time goes:
time: 2060 us; the launch traced here: 2050 us
  waiting for transfers between devices  1160 us (56%)
  matrix products  413 us (20%)
  other arithmetic  183 us (9%)
  local copies, waits for them, and re-layouts  169 us (8%)
  blocking collectives  104 us (5%)
    reduce_scatter x1, waiting for transfers between devices, body(): lax.psum_scatter(down_grad.astype(jnp.bfloat16), 'fsdp', scatter_dimensio...  166 us
    reduce_scatter x1, waiting for transfers between devices, body(): lax.psum_scatter(up_grad.astype(jnp.bfloat16), 'fsdp', scatter_dimension=...  166 us
    reduce_scatter x1, waiting for transfers between devices, body(): lax.psum_scatter(gate_grad.astype(jnp.bfloat16), 'fsdp', scatter_dimensio...  166 us
    all_gather x1, waiting for transfers between devices, body(): lax.all_gather(up_weight, 'fsdp', axis=0, tiled=True)  127 us
    all_gather x1, waiting for transfers between devices, body(): lax.all_gather(down_weight, 'fsdp', axis=0, tiled=True)  127 us
    convert_element_type x8, other arithmetic, backward_group(): grad_scores = (probs * (grad_probs - delta)).astype(jnp.bfloat16)  88.3 us
    dot_general x16, matrix products, scores_of(): jnp.einsum('thd,ld->htl', query_part, key_part, preferred_element_type=jn...  83.8 us
    reduce_scatter x1, waiting for transfers between devices, body(): lax.psum_scatter(out_grad.astype(jnp.bfloat16), 'fsdp', scatter_dimension...  70.3 us
  transfers between devices with their start and end apart: 19, of which 18 were waited for; matrix products, arithmetic and copies ran while one was open for 13% of the time, Pallas kernels for 0%

commit v1 on v0

v1 whole, which is shorter than its diff:
```python
import jax
import jax.numpy as jnp
from jax import lax
from jax.experimental import pallas as pl
from jax.experimental.pallas import tpu as pltpu
from jax.sharding import PartitionSpec as P

epsilon = 1e-05
theta_base = 1000000.0


def rotary_tables(positions, width):
    half_width = width // 2
    freqs = theta_base ** (-jnp.arange(half_width, dtype=jnp.float32) * 2.0 / width)
    angles = positions.astype(jnp.float32)[:, None] * freqs[None, :]
    return (jnp.cos(angles)[:, None, :], jnp.sin(angles)[:, None, :])


def rotate(values, cosine, sine):
    half_width = values.shape[-1] // 2
    first_half = values[..., :half_width]
    second_half = values[..., half_width:]
    return jnp.concatenate(
        [first_half * cosine - second_half * sine, second_half * cosine + first_half * sine],
        axis=-1,
    )


def unrotate(grads, cosine, sine):
    half_width = grads.shape[-1] // 2
    first_half = grads[..., :half_width]
    second_half = grads[..., half_width:]
    return jnp.concatenate(
        [first_half * cosine + second_half * sine, second_half * cosine - first_half * sine],
        axis=-1,
    )


def head_norm(values, gain_vector):
    inverse = lax.rsqrt(jnp.mean(values * values, axis=-1, keepdims=True) + epsilon)
    unit_values = values * inverse
    return (unit_values * gain_vector, unit_values, inverse)


def norm_back(upstream, unit_values, inverse, gain_vector):
    scaled = upstream * gain_vector
    grad_in = inverse * (
        scaled - unit_values * jnp.mean(scaled * unit_values, axis=-1, keepdims=True)
    )
    return (grad_in, upstream * unit_values)


def outer_product(left, right):
    return lax.dot_general(
        left, right, (((0,), (0,)), ((), ())), preferred_element_type=jnp.float32
    )


def times_transposed(left, right):
    return lax.dot_general(
        left, right, (((1,), (1,)), ((), ())), preferred_element_type=jnp.float32
    )


def gather_rows(shard):
    part = shard.shape[0] // lax.axis_size("ctx")
    own = lax.dynamic_slice_in_dim(shard, lax.axis_index("ctx") * part, part, 0)
    return lax.all_gather(own, ("fsdp", "ctx"), axis=0, tiled=True)


def halve_over_ctx(parts):
    count = lax.axis_size("ctx")
    me = lax.axis_index("ctx")
    step = 1
    while step < count:
        lead, left, rows, width = parts.shape
        pairs = parts.reshape(lead, left // 2, 2, rows, width)
        bit = (me // step) % 2
        keep = lax.dynamic_index_in_dim(pairs, bit, 2, keepdims=False)
        send = lax.dynamic_index_in_dim(pairs, 1 - bit, 2, keepdims=False)
        got = lax.ppermute(send, "ctx", [(i, i ^ step) for i in range(count)])
        parts = (keep.astype(jnp.float32) + got.astype(jnp.float32)).astype(jnp.bfloat16)
        step *= 2
    return parts[:, 0]


def scatter_rows(grad):
    owners, count = lax.axis_size("fsdp"), lax.axis_size("ctx")
    rows, width = grad.shape
    part = rows // (owners * count)
    mine = halve_over_ctx(grad.reshape(owners, count, part, width))
    mine = lax.psum_scatter(
        mine.reshape(owners * part, width), "fsdp", scatter_dimension=0, tiled=True
    )
    return lax.all_gather(mine, "ctx", axis=0, tiled=True).astype(jnp.float32)


def place(values, side):
    blank = jnp.zeros_like(values)
    return jnp.concatenate([values, blank] if side == 0 else [blank, values], axis=1)


def stacked(ref, rows, side):
    first = ref[rows, 128 * side : 128 * side + 64]
    second = ref[rows, 128 * side + 64 : 128 * side + 128]
    return jnp.concatenate([place(first, side), place(second, side)], axis=0)


def causal(half_block):
    shape = (half_block, 2 * half_block)
    key_at = lax.broadcasted_iota(jnp.int32, shape, 0)
    query_at = lax.broadcasted_iota(jnp.int32, shape, 1)
    query_at = jnp.where(query_at >= half_block, query_at - half_block, query_at)
    return query_at >= key_at


def dot_first(left, right):
    return lax.dot_general(
        left, right, (((0,), (0,)), ((), ())), preferred_element_type=jnp.float32
    )


def forward_kernel(place_ref, q_ref, k_ref, v_ref, mixed_ref, inverse_ref):
    half_block = q_ref.shape[0] // 2
    blocks = k_ref.shape[0] // half_block
    lane = lax.broadcasted_iota(jnp.int32, (half_block, 128), 1)
    for half in range(2):
        rows = slice(half * half_block, (half + 1) * half_block)
        last = place_ref[blocks + half]
        outs = []
        for side in range(2):
            queries = stacked(q_ref, rows, side) * jnp.bfloat16(0.125)
            own_lane = (lane < 64) if side == 0 else (lane >= 64)

            def step(j, acc, diagonal=False):
                at = pl.ds(pl.multiple_of(place_ref[j] * half_block, half_block), half_block)
                expo = jnp.exp(times_transposed(k_ref[at, :], queries))
                if diagonal:
                    expo = jnp.where(causal(half_block), expo, 0.0)
                value_one = jnp.where(own_lane, v_ref[at, :], jnp.bfloat16(1))
                return acc + dot_first(value_one, expo.astype(jnp.bfloat16))

            acc = jnp.zeros((128, 2 * half_block), jnp.float32)
            acc = lax.fori_loop(0, last, step, acc)
            acc = step(last, acc, True)
            inverse = 1.0 / acc[64 * (1 - side) : 64 * (1 - side) + 1, :]
            out = acc[64 * side : 64 * side + 64, :] * inverse
            for head in range(2):
                cols = slice(head * half_block, (head + 1) * half_block)
                outs.append(out[:, cols])
                at_head = 2 * side + head
                inverse_ref[0, at_head : at_head + 1, rows] = inverse[:, cols]
        mixed_ref[rows, :] = jnp.concatenate(outs, axis=0).T.astype(jnp.bfloat16)


def backward_kernel(
    place_ref, q_ref, k_ref, v_ref, g_ref, inverse_ref, delta_ref, dq_ref, dk_ref, dv_ref, dk, dv
):
    half_block = q_ref.shape[0] // 2
    blocks = k_ref.shape[0] // half_block
    dk[...] = jnp.zeros_like(dk)
    dv[...] = jnp.zeros_like(dv)
    for half in range(2):
        rows = slice(half * half_block, (half + 1) * half_block)
        last = place_ref[blocks + half]
        outs = []
        for side in range(2):
            queries = stacked(q_ref, rows, side) * jnp.bfloat16(0.125)
            upstream = stacked(g_ref, rows, side)
            inverse, delta = (
                jnp.concatenate(
                    [ref[0, 2 * side + head : 2 * side + head + 1, rows] for head in range(2)],
                    axis=1,
                )
                for ref in (inverse_ref, delta_ref)
            )

            def step(j, acc, diagonal=False):
                at = pl.ds(pl.multiple_of(place_ref[j] * half_block, half_block), half_block)
                keys = k_ref[at, :]
                probs = jnp.exp(times_transposed(keys, queries)) * inverse
                if diagonal:
                    probs = jnp.where(causal(half_block), probs, 0.0)
                grad_probs = times_transposed(v_ref[at, :], upstream)
                grad_scores = (probs * (grad_probs - delta)).astype(jnp.bfloat16)
                dk[at, :] += jnp.dot(grad_scores, queries, preferred_element_type=jnp.float32)
                dv[at, :] += jnp.dot(
                    probs.astype(jnp.bfloat16), upstream, preferred_element_type=jnp.float32
                )
                return acc + dot_first(keys, grad_scores)

            acc = jnp.zeros((128, 2 * half_block), jnp.float32)
            acc = lax.fori_loop(0, last, step, acc)
            acc = step(last, acc, True)
            for head in range(2):
                outs.append(
                    acc[64 * side : 64 * side + 64, head * half_block : (head + 1) * half_block]
                )
        dq_ref[rows, :] = jnp.concatenate(outs, axis=0).T * 0.125
    dk_ref[...] = dk[...].astype(dk_ref.dtype)
    dv_ref[...] = dv[...].astype(dv_ref.dtype)


def attention_specs(tokens, length):
    query_spec = pl.BlockSpec((tokens, 256), lambda i, _: (0, i))
    key_spec = pl.BlockSpec((length, 128), lambda i, _: (0, i))
    row_spec = pl.BlockSpec((1, 4, tokens), lambda i, _: (i, 0, 0))
    return query_spec, key_spec, row_spec


def attend(places, queries, keys, values):
    tokens, length = queries.shape[0], keys.shape[0]
    pairs = keys.shape[1] // 128
    query_spec, key_spec, row_spec = attention_specs(tokens, length)
    work = 4 * pairs * tokens * (length + 2 * tokens)
    return pl.pallas_call(
        forward_kernel,
        grid_spec=pltpu.PrefetchScalarGridSpec(
            num_scalar_prefetch=1,
            grid=(pairs,),
            in_specs=[query_spec, key_spec, key_spec],
            out_specs=[query_spec, row_spec],
        ),
        out_shape=[
            jax.ShapeDtypeStruct(queries.shape, jnp.bfloat16),
            jax.ShapeDtypeStruct((pairs, 4, tokens), jnp.float32),
        ],
        compiler_params=pltpu.CompilerParams(vmem_limit_bytes=32 * 2**20),
        cost_estimate=pl.CostEstimate(
            flops=work * 256, bytes_accessed=12 * 2**20, transcendentals=work
        ),
        name="attention_forward",
    )(places, queries, keys, values)


def attend_back(places, queries, keys, values, upstream, inverse, delta):
    tokens, length = queries.shape[0], keys.shape[0]
    pairs = keys.shape[1] // 128
    query_spec, key_spec, row_spec = attention_specs(tokens, length)
    work = 4 * pairs * tokens * (length + 2 * tokens)
    return pl.pallas_call(
        backward_kernel,
        grid_spec=pltpu.PrefetchScalarGridSpec(
            num_scalar_prefetch=1,
            grid=(pairs,),
            in_specs=[query_spec, key_spec, key_spec, query_spec, row_spec, row_spec],
            out_specs=[query_spec, key_spec, key_spec],
            scratch_shapes=[pltpu.VMEM((length, 128), jnp.float32)] * 2,
        ),
        out_shape=[
            jax.ShapeDtypeStruct(queries.shape, jnp.float32),
            jax.ShapeDtypeStruct(keys.shape, jnp.bfloat16),
            jax.ShapeDtypeStruct(keys.shape, jnp.bfloat16),
        ],
        compiler_params=pltpu.CompilerParams(vmem_limit_bytes=32 * 2**20),
        cost_estimate=pl.CostEstimate(
            flops=work * 640, bytes_accessed=16 * 2**20, transcendentals=work
        ),
        name="attention_backward",
    )(places, queries, keys, values, upstream, inverse, delta)


def body(
    inputs,
    cotangent,
    block_table,
    attn_gain,
    query_weight,
    key_weight,
    value_weight,
    query_gain,
    key_gain,
    out_weight,
    ffn_gain,
    gate_weight,
    up_weight,
    down_weight,
):
    width_q, width_k = query_weight.shape[1], key_weight.shape[1]
    gains = jnp.pad(jnp.stack([attn_gain, ffn_gain], axis=1), ((0, 0), (0, 126)))
    w_first = gather_rows(
        jnp.concatenate([query_weight, key_weight, value_weight, gains], axis=1)
    )
    w_query = w_first[:, :width_q]
    w_key = w_first[:, width_q : width_q + width_k]
    w_value = w_first[:, width_q + width_k : width_q + 2 * width_k]
    gain_attn_low = w_first[:, width_q + 2 * width_k]
    gain_ffn_low = w_first[:, width_q + 2 * width_k + 1]
    w_out = gather_rows(out_weight)
    w_gate, w_up, w_down = (
        gather_rows(gate_weight),
        gather_rows(up_weight),
        gather_rows(down_weight),
    )
    gain_attn = gain_attn_low.astype(jnp.float32)
    gain_ffn = gain_ffn_low.astype(jnp.float32)
    gain_query = query_gain.astype(jnp.float32)
    gain_key = key_gain.astype(jnp.float32)
    head_width = query_gain.shape[0]
    heads_count = w_query.shape[1] // head_width
    kv_count = w_key.shape[1] // head_width
    tokens = inputs.shape[1]
    half_block = tokens // 2
    table_row = block_table[0]
    block_count = table_row.shape[0]
    own_blocks = lax.dynamic_slice_in_dim(table_row, 2 * lax.axis_index("ctx"), 2)
    offsets = jnp.arange(half_block, dtype=jnp.int32)
    own_positions = (own_blocks[:, None] * half_block + offsets[None, :]).reshape(-1)
    slot_ids = jnp.arange(block_count, dtype=jnp.int32)
    slot_of_block = jnp.sum(
        jnp.where(table_row[None, :] == slot_ids[:, None], slot_ids[None, :], 0), axis=1
    )
    places = jnp.concatenate([slot_of_block, own_blocks])
    hidden_in = inputs[0].astype(jnp.float32)
    inverse_one = lax.rsqrt(jnp.mean(hidden_in * hidden_in, axis=-1, keepdims=True) + epsilon)
    unit_one = hidden_in * inverse_one
    normed = (unit_one * gain_attn).astype(jnp.bfloat16)
    q_raw = jnp.dot(normed, w_query, preferred_element_type=jnp.float32)
    k_raw = jnp.dot(normed, w_key, preferred_element_type=jnp.float32)
    values_low = jnp.dot(normed, w_value, preferred_element_type=jnp.float32).astype(jnp.bfloat16)
    cosine, sine = rotary_tables(own_positions, head_width)
    q_normed, q_unit, q_inverse = head_norm(
        q_raw.reshape(tokens, heads_count, head_width), gain_query
    )
    k_normed, k_unit, k_inverse = head_norm(k_raw.reshape(tokens, kv_count, head_width), gain_key)
    queries = (
        rotate(q_normed, cosine, sine)
        .reshape(tokens, heads_count * head_width)
        .astype(jnp.bfloat16)
    )
    keys_low = (
        rotate(k_normed, cosine, sine).reshape(tokens, kv_count * head_width).astype(jnp.bfloat16)
    )
    key_value = lax.all_gather(
        jnp.concatenate([keys_low, values_low], axis=1), "ctx", axis=0, tiled=True
    )
    key_all, value_all = key_value[:, :width_k], key_value[:, width_k:]
    mixed, inverse_sums = attend(places, queries, key_all, value_all)
    resid = hidden_in + jnp.dot(mixed, w_out, preferred_element_type=jnp.float32)
    inverse_two = lax.rsqrt(jnp.mean(resid * resid, axis=-1, keepdims=True) + epsilon)
    unit_two = resid * inverse_two
    ffn_in = (unit_two * gain_ffn).astype(jnp.bfloat16)
    gate = jnp.dot(ffn_in, w_gate, preferred_element_type=jnp.float32)
    up_part = jnp.dot(ffn_in, w_up, preferred_element_type=jnp.float32)
    sigma = jax.nn.sigmoid(gate)
    silu_gate = gate * sigma
    hidden = (silu_gate * up_part).astype(jnp.bfloat16)
    output = (resid + jnp.dot(hidden, w_down, preferred_element_type=jnp.float32)).astype(
        jnp.bfloat16
    )
    grad_out = cotangent[0]
    down_grad = outer_product(hidden, grad_out)
    grad_hidden = times_transposed(grad_out, w_down)
    grad_gate = (grad_hidden * up_part * sigma * (1.0 + gate * (1.0 - sigma))).astype(jnp.bfloat16)
    grad_up = (grad_hidden * silu_gate).astype(jnp.bfloat16)
    gate_grad = outer_product(ffn_in, grad_gate)
    up_grad = outer_product(ffn_in, grad_up)
    grad_ffn_in = times_transposed(grad_gate, w_gate) + times_transposed(grad_up, w_up)
    grad_resid_norm, ffn_gain_terms = norm_back(grad_ffn_in, unit_two, inverse_two, gain_ffn)
    ffn_gain_sum = jnp.sum(ffn_gain_terms, axis=0)
    grad_resid = grad_out.astype(jnp.float32) + grad_resid_norm
    grad_attn = grad_resid.astype(jnp.bfloat16)
    out_grad = outer_product(mixed, grad_attn)
    grad_mixed = times_transposed(grad_attn, w_out).astype(jnp.bfloat16)

    delta = jnp.sum(
        (mixed.astype(jnp.float32) * grad_mixed.astype(jnp.float32)).reshape(
            tokens, heads_count, head_width
        ),
        axis=-1,
    ).T.reshape(inverse_sums.shape)
    grad_queries, grad_keys_all, grad_values_all = attend_back(
        places, queries, key_all, value_all, grad_mixed, inverse_sums, delta
    )
    grad_own = halve_over_ctx(
        jnp.concatenate([grad_keys_all, grad_values_all], axis=1).reshape(
            1, lax.axis_size("ctx"), tokens, 2 * width_k
        )
    )[0].astype(jnp.float32)
    grad_keys_own, grad_values_own = grad_own[:, :width_k], grad_own[:, width_k:]
    grad_q_normed = unrotate(grad_queries.reshape(tokens, heads_count, head_width), cosine, sine)
    grad_q_raw, query_gain_terms = norm_back(grad_q_normed, q_unit, q_inverse, gain_query)
    grad_k_normed = unrotate(grad_keys_own.reshape(tokens, kv_count, head_width), cosine, sine)
    grad_k_raw, key_gain_terms = norm_back(grad_k_normed, k_unit, k_inverse, gain_key)
    grad_q_low = grad_q_raw.reshape(tokens, heads_count * head_width).astype(jnp.bfloat16)
    grad_k_low = grad_k_raw.reshape(tokens, kv_count * head_width).astype(jnp.bfloat16)
    grad_v_low = grad_values_own.astype(jnp.bfloat16)
    first_grad = outer_product(
        normed, jnp.concatenate([grad_q_low, grad_k_low, grad_v_low], axis=1)
    )
    grad_normed = (
        times_transposed(grad_q_low, w_query)
        + times_transposed(grad_k_low, w_key)
        + times_transposed(grad_v_low, w_value)
    )
    grad_input_norm, attn_gain_terms = norm_back(grad_normed, unit_one, inverse_one, gain_attn)
    input_grad = (grad_resid + grad_input_norm).astype(jnp.bfloat16)
    attn_gain_sum = jnp.sum(attn_gain_terms, axis=0)
    down_owned, gate_owned, up_owned, out_owned, first_owned = (
        scatter_rows(grad.astype(jnp.bfloat16))
        for grad in (down_grad, gate_grad, up_grad, out_grad, first_grad)
    )
    width = attn_gain_sum.shape[0]
    gain_sums = lax.psum(
        jnp.concatenate(
            [
                attn_gain_sum,
                ffn_gain_sum,
                jnp.sum(query_gain_terms, axis=(0, 1)),
                jnp.sum(key_gain_terms, axis=(0, 1)),
            ]
        ),
        ("ctx", "fsdp"),
    )
    own_gain = lax.axis_index("fsdp") * attn_gain.shape[0]
    attn_owned = lax.dynamic_slice_in_dim(gain_sums, own_gain, attn_gain.shape[0])
    ffn_owned = lax.dynamic_slice_in_dim(gain_sums, width + own_gain, attn_gain.shape[0])
    query_gain_grad = gain_sums[2 * width : 2 * width + head_width]
    key_gain_grad = gain_sums[2 * width + head_width :]
    return (
        output[None],
        input_grad[None],
        attn_owned,
        first_owned[:, :width_q],
        first_owned[:, width_q : width_q + width_k],
        first_owned[:, width_q + width_k :],
        query_gain_grad,
        key_gain_grad,
        out_owned,
        ffn_owned,
        gate_owned,
        up_owned,
        down_owned,
    )


def solution(mesh):
    return jax.shard_map(
        body,
        mesh=mesh,
        in_specs=(
            P("fsdp", "ctx", None),
            P("fsdp", "ctx", None),
            P("fsdp", None),
            P("fsdp"),
            P("fsdp", None),
            P("fsdp", None),
            P("fsdp", None),
            P(),
            P(),
            P("fsdp", None),
            P("fsdp"),
            P("fsdp", None),
            P("fsdp", None),
            P("fsdp", None),
        ),
        out_specs=(
            P("fsdp", "ctx", None),
            P("fsdp", "ctx", None),
            P("fsdp"),
            P("fsdp", None),
            P("fsdp", None),
            P("fsdp", None),
            P(),
            P(),
            P("fsdp", None),
            P("fsdp"),
            P("fsdp", None),
            P("fsdp", None),
            P("fsdp", None),
        ),
        check_vma=False,
    )
```

time: 2060 us -> 964 us (0.47)
  waiting for transfers between devices: 1160 us -> 541 us
  matrix products: 413 us -> 124 us
  other arithmetic: 183 us -> 67 us
  local copies, waits for them, and re-layouts: 169 us -> 73.3 us
  Pallas kernels: 0 us -> 75.6 us
  blocking collectives: 104 us -> 53.3 us
    reduce_scatter x9 -> x5, waiting for transfers between devices: 781 us -> 24.6 us  [scatter_rows(): lax.psum_scatter(mine.reshape(owners * part, width), 'fsdp', scatter_dime...]
    dot_general x56 -> x0, matrix products: 288 us -> none  [the longest x16 83.8 us: scores_of(): jnp.einsum('thd,ld->htl', query_part, key_part, preferred_element_type=jn...]
    ppermute x0 -> x12, waiting for transfers between devices: none -> 147 us  [halve_over_ctx(): got = lax.ppermute(send, 'ctx', [(i, i ^ step) for i in range(count)])]
    pallas_call x0 -> x2, Pallas kernels: none -> 75.6 us  [the longest x1 44.3 us: attend_back(): pl.pallas_call(backward_kernel, grid_spec=pltpu.PrefetchScalarGridSpec(nu...]
    gather x7 -> x0, local copies, waits for them, and re-layouts: 67 us -> none  [the longest x2 23.7 us: back_to_rows(): jnp.take(window_grad, first_index, axis=0)]
    convert_element_type x20 -> x16, other arithmetic: 107 us -> 44.4 us  [the longest x11 33.1 us: halve_over_ctx(): (keep.astype(jnp.float32) + got.astype(jnp.float32)).astype(jnp.bfloat16)]
    while x34 -> x0, local copies, waits for them, and re-layouts: 43 us -> none
    and x18 -> x0, other arithmetic: 31.7 us -> none  [the longest x16 30.5 us: body(): (own_positions[:, None] >= window_pos[None, :]) & (lower_query[:, None] =...]
  transfers between devices with their start and end apart: 19 -> 26, of which waited for: 18 -> 17; matrix products, arithmetic and copies ran while one was open for 13% -> 20% of each run, Pallas kernels for 0% -> 8%
where the time goes in v1:
time: 964 us; the launch traced here: 959 us
  waiting for transfers between devices  541 us (56%)
  matrix products  124 us (13%)
  Pallas kernels  75.6 us (8%)
  local copies, waits for them, and re-layouts  73.3 us (8%)
  other arithmetic  67 us (7%)
  blocking collectives  53.3 us (6%)
  between operations  15.1 us (2%)
  starting transfers between devices  9.74 us (1%)
    all_gather x5, waiting for transfers between devices, gather_rows(): return lax.all_gather(own, ('fsdp', 'ctx'), axis=0, tiled=True)  313 us
    ppermute x12, waiting for transfers between devices, halve_over_ctx(): got = lax.ppermute(send, 'ctx', [(i, i ^ step) for i in range(count)])  147 us
    dot_general x7, matrix products, times_transposed(): lax.dot_general(left, right, (((1,), (1,)), ((), ())), preferred_element_...  52.7 us
    pallas_call x1, Pallas kernels, attend_back(): pl.pallas_call(backward_kernel, grid_spec=pltpu.PrefetchScalarGridSpec(nu...  44.3 us
    all_gather x3, waiting for transfers between devices, scatter_rows(): return lax.all_gather(mine, 'ctx', axis=0, tiled=True).astype(jnp.float32)  41 us
    psum x1, blocking collectives, body(): lax.psum(jnp.concatenate([attn_gain_sum, ffn_gain_sum, jnp.sum(query_gain...  40 us
    convert_element_type x11, other arithmetic, halve_over_ctx(): (keep.astype(jnp.float32) + got.astype(jnp.float32)).astype(jnp.bfloat16)  33.1 us
    pallas_call x1, Pallas kernels, attend(): pl.pallas_call(forward_kernel, grid_spec=pltpu.PrefetchScalarGridSpec(num...  31.3 us
  transfers between devices with their start and end apart: 26, of which 17 were waited for; matrix products, arithmetic and copies ran while one was open for 20% of the time, Pallas kernels for 8%

profile of v1, /device:TPU:0, one launch (start us, length us, event | category | flops | bytes accessed | tf_op | source)
XLA Modules:
  0.0 959.0 jit_solution(371885430273159002)
XLA Ops:
  13.1 64.1 %all-gather.10.cloned.1.call-done = bf16[1024,2176]{1,0:T(8,128)(2,1)} async-done(((bf16[32,2176]{1,0:T(8,128)(2,1)}), bf16[1024,2176]{1,0:T(8,128)(2,1)}) %all-gather.10.cloned.1.call-update) | async-done | bytes 4456464 | tf_op jit(solution)/shard_map/all_gather | solution.py:68
  81.2 2.1 multiply_reduce_fusion.8
  84.5 2.0 convolution_convert_fusion.6
  94.4 3.6 slice_bitcast_fusion
  98.0 3.9 copy.51
  101.9 3.0 multiply_reduce_fusion.5
  107.2 13.4 %all-gather.12.cloned.1.call-done = bf16[2048,1024]{1,0:T(8,128)(2,1)} async-done(((bf16[512,1024]{1,0:T(8,128)(2,1)}), bf16[2048,1024]{1,0:T(8,128)(2,1)}) %all-gather.12.cloned.1.call-update) | async-done | bytes 4194320 | tf_op jit(solution)/shard_map/all_gather | solution.py:334
  120.6 2.5 fusion.62
  123.1 31.3 %attention_forward.1 = (bf16[512,1024]{1,0:T(8,128)(2,1)S(1)}, f32[4,4,512]{2,1,0:T(4,128)S(1)}) custom-call(s32[10]{0:T(128)S(1)} %pad_add_fusion.place_ref, bf16[512,1024]{1,0:T(8,128)(2,1)S(1)} %copy.55.q_ref, bf16[2048,512]{1,0:T(8,128)(2,1)S(1)} %get-tuple-element.39.k_ref, bf16[2048,512]{1,0:T(8,128)(2,1)S(1)} %get-tuple-element.38.v_ref), custom_call_target="tpu_custom_call" | custom-call | flops 6442450944 | bytes 12582912 | tf_op jit(solution)/shard_map/attention_forward/pallas_call | solution.py:216
  157.1 23.7 %all-gather.14.cloned.1.call-done = bf16[1024,1024]{1,0:T(8,128)(2,1)} async-done(((bf16[32,1024]{1,0:T(8,128)(2,1)}), bf16[1024,1024]{1,0:T(8,128)(2,1)}) %all-gather.14.cloned.1.call-update) | async-done | bytes 2097168 | tf_op jit(solution)/shard_map/all_gather | solution.py:68
  180.8 2.9 multiply_reduce_fusion.4
  185.4 79.7 %all-gather.16.cloned.1.call-done = bf16[1024,4608]{1,0:T(8,128)(2,1)} async-done(((bf16[32,4608]{1,0:T(8,128)(2,1)}), bf16[1024,4608]{1,0:T(8,128)(2,1)}) %all-gather.16.cloned.1.call-update) | async-done | bytes 9437200 | tf_op jit(solution)/shard_map/all_gather | solution.py:68
  265.1 11.1 %fusion.67 = f32[512,4608]{1,0:T(8,128)} fusion(bf16[512,1024]{1,0:T(8,128)(2,1)S(1)} %multiply_convert_fusion.2, bf16[1024,4608]{1,0:T(8,128)(2,1)} %all-gather.16.cloned.1.call-done), kind=kOutput, calls=%fused_computation.165 | convolution fusion | flops 4831838208 | bytes 19922944 | tf_op jit(solution)/shard_map/dot_general | solution.py:343
  276.2 72.9 %all-gather.18.cloned.1.call-done = bf16[1024,4608]{1,0:T(8,128)(2,1)} async-done(((bf16[32,4608]{1,0:T(8,128)(2,1)}), bf16[1024,4608]{1,0:T(8,128)(2,1)}) %all-gather.18.cloned.1.call-update) | async-done | bytes 9437200 | tf_op jit(solution)/shard_map/all_gather | solution.py:68
  349.1 11.1 %fusion.68 = f32[512,4608]{1,0:T(8,128)} fusion(bf16[512,1024]{1,0:T(8,128)(2,1)S(1)} %multiply_convert_fusion.2, bf16[1024,4608]{1,0:T(8,128)(2,1)} %all-gather.18.cloned.1.call-done), kind=kOutput, calls=%fused_computation.166 | convolution fusion | flops 4831838208 | bytes 19922944 | tf_op jit(solution)/shard_map/dot_general | solution.py:344
  360.2 72.8 %all-gather.20.cloned.1.call-done = bf16[4608,1024]{1,0:T(8,128)(2,1)} async-done(((bf16[144,1024]{1,0:T(8,128)(2,1)}), bf16[4608,1024]{1,0:T(8,128)(2,1)}) %all-gather.20.cloned.1.call-update) | async-done | bytes 9437200 | tf_op jit(solution)/shard_map/all_gather | solution.py:68
  433.1 18.1 %fusion.6 = (bf16[512,4608]{1,0:T(8,128)(2,1)}, bf16[512,4608]{1,0:T(8,128)(2,1)}, bf16[512,4608]{1,0:T(8,128)(2,1)}) fusion(f32[512,4608]{1,0:T(8,128)} %fusion.67, f32[512,4608]{1,0:T(8,128)} %fusion.68, bf16[4608,1024]{1,0:T(8,128)(2,1)} %all-gather.20.cloned.1.call-done, bf16[1,512,1024]{2,1,0:T(8,128)(2,1)} %param.15), kind=kOutput, calls=%fused_computation.14 | convolution fusion | flops 4867227648 | bytes 43515904 | tf_op jit(solution)/shard_map/dot_general | solution.py:60
  451.1 7.7 convolution_convert_fusion.2
  458.8 2.8 dynamic-slice_bitcast_fusion.2
  461.6 2.2 copy-done.24
  464.1 7.8 convolution_convert_fusion.1
  471.9 2.5 dynamic-slice_bitcast_fusion.1
  474.4 2.6 copy-done.25
  477.3 3.7 fusion.2
  482.7 9.4 fusion.69
  492.1 8.9 multiply_reduce_fusion.1
  501.1 33.6 %collective-permute-done.7 = bf16[8,1,32,4608]{3,2,1,0:T(8,128)(2,1)S(1)} collective-permute-done((bf16[8,1,32,4608]{3,2,1,0:T(8,128)(2,1)S(1)}, bf16[8,1,32,4608]{3,2,1,0:T(8,128)(2,1)S(1)}, u32[]{:S(2)}, u32[]{:S(2)}) %collective-permute-start.7) | collective-permute-done | bytes 2359328 | tf_op jit(solution)/shard_map/ppermute | solution.py:81
  534.7 2.1 add_convert_fusion.2
  536.9 5.3 fusion.1
  548.8 3.0 convert_multiply_fusion.1
  551.8 2.9 copy.57
  554.7 2.0 bitcast_reduce_fusion
  556.7 8.0 convolution_convert_fusion
  564.7 3.1 dynamic-slice_bitcast_fusion
  569.7 29.0 %collective-permute-done.9 = bf16[8,1,32,4608]{3,2,1,0:T(8,128)(2,1)} collective-permute-done((bf16[8,1,32,4608]{3,2,1,0:T(8,128)(2,1)}, bf16[8,1,32,4608]{3,2,1,0:T(8,128)(2,1)}, u32[]{:S(2)}, u32[]{:S(2)}) %collective-permute-start.9) | collective-permute-done | bytes 2359328 | tf_op jit(solution)/shard_map/ppermute | solution.py:81
  598.6 3.7 add_convert_fusion.1
  606.8 44.3 %attention_backward.1 = (f32[512,1024]{1,0:T(8,128)S(1)}, bf16[2048,512]{1,0:T(8,128)(2,1)S(1)}, bf16[2048,512]{1,0:T(8,128)(2,1)S(1)}) custom-call(s32[10]{0:T(128)S(1)} %pad_add_fusion.place_ref, bf16[512,1024]{1,0:T(8,128)(2,1)S(1)} %copy.55.q_ref, bf16[2048,512]{1,0:T(8,128)(2,1)S(1)} %copy-done.5, bf16[2048,512]{1,0:T(8,128)(2,1)S(1)} %copy-done.3, ...), custom_call_target="tpu_custom_call" | custom-call | flops 16106127360 | bytes 16777216 | tf_op jit(solution)/shard_map/attention_backward/pallas_call | solution.py:241
  661.5 2.0 multiply_add_fusion.1
  665.3 2.0 fusion.32
  668.9 2.6 fusion.9
  673.1 6.3 fusion
  686.5 18.2 %collective-permute-done.1 = bf16[1,1,512,1024]{3,2,1,0:T(8,128)(2,1)} collective-permute-done((bf16[1,1,512,1024]{3,2,1,0:T(8,128)(2,1)}, bf16[1,1,512,1024]{3,2,1,0:T(8,128)(2,1)}, u32[]{:S(2)}, u32[]{:S(2)}) %collective-permute-start.1) | collective-permute-done | bytes 1048608 | tf_op jit(solution)/shard_map/ppermute | solution.py:81
  707.8 2.1 copy.61
  711.8 4.6 convolution_convert_fusion.3
  716.4 38.4 %collective-permute-done.11 = bf16[8,1,144,1024]{3,2,1,0:T(8,128)(2,1)} collective-permute-done((bf16[8,1,144,1024]{3,2,1,0:T(8,128)(2,1)}, bf16[8,1,144,1024]{3,2,1,0:T(8,128)(2,1)}, u32[]{:S(2)}, u32[]{:S(2)}) %collective-permute-start.11) | collective-permute-done | bytes 2359328 | tf_op jit(solution)/shard_map/ppermute | solution.py:81
  754.9 4.2 add_convert_fusion
  761.1 4.1 collective-permute-done.2
  767.8 23.8 %collective-permute-done.3 = bf16[8,1,32,2048]{3,2,1,0:T(8,128)(2,1)S(1)} collective-permute-done((bf16[8,1,32,2048]{3,2,1,0:T(8,128)(2,1)S(1)}, bf16[8,1,32,2048]{3,2,1,0:T(8,128)(2,1)S(1)}, u32[]{:S(2)}, u32[]{:S(2)}) %collective-permute-start.3) | collective-permute-done | bytes 1048608 | tf_op jit(solution)/shard_map/ppermute | solution.py:81
  794.4 4.7 fusion.33
  799.1 9.8 %fusion.35 = bf16[1,512,1024]{2,1,0:T(8,128)(2,1)} fusion(f32[512,1024]{1,0:T(8,128)S(1)} %copy-done.29, bf16[512,4608]{1,0:T(8,128)(2,1)} %get-tuple-element.37, bf16[4608,1024]{1,0:T(8,128)(2,1)} %all-gather.20.cloned.1.call-done), kind=kOutput, calls=%fused_computation.81 | convolution fusion | flops 4832886784 | bytes 17301504 | tf_op jit(solution)/shard_map/dot_general | solution.py:348
  808.9 6.0 all_gather.40
  815.8 3.5 fusion.44
  819.2 7.8 reduce-scatter.14.cloned.1.call-done
  827.0 5.2 fusion.23
  832.3 40.0 %psum.7 = f32[2176]{0:T(1024)S(1)} all-reduce(f32[2176]{0:T(1024)S(1)} %concatenate.40), channel_id=1, replica_groups=mesh['ctx'=4,'fsdp'=8] {'ctx','fsdp'}, use_global_device_ids=true, to_apply=%region_14.15 | all-reduce | flops 2176 | bytes 17408 | tf_op jit(solution)/shard_map/psum | solution.py:404
  873.5 3.1 fusion.38
  876.6 16.8 %reduce-scatter.6.cloned.1.call-done = bf16[32,2048]{1,0:T(8,128)(2,1)} async-done(((bf16[256,2048]{1,0:T(8,128)(2,1)}), bf16[32,2048]{1,0:T(8,128)(2,1)}) %reduce-scatter.6.cloned.1.call-update) | async-done | bytes 131088 | tf_op jit(solution)/shard_map/reduce_scatter | solution.py:92
  893.4 7.3 all_gather.39
  902.4 8.9 all-gather.22.cloned.1.call-done
  911.3 2.9 convert_element_type.359
  914.2 16.1 %all-gather.24.cloned.1.call-done = bf16[128,4608]{1,0:T(8,128)(2,1)} async-done(((bf16[32,4608]{1,0:T(8,128)(2,1)}), bf16[128,4608]{1,0:T(8,128)(2,1)}) %all-gather.24.cloned.1.call-update) | async-done | bytes 1179664 | tf_op jit(solution)/shard_map/all_gather | solution.py:95
  930.4 3.0 convert_element_type.368
  933.4 15.9 %all-gather.26.cloned.1.call-done = bf16[576,1024]{1,0:T(8,128)(2,1)} async-done(((bf16[144,1024]{1,0:T(8,128)(2,1)}), bf16[576,1024]{1,0:T(8,128)(2,1)}) %all-gather.26.cloned.1.call-update) | async-done | bytes 1179664 | tf_op jit(solution)/shard_map/all_gather | solution.py:95
  949.3 3.0 convert_element_type.377
  (254 shorter events, 78.9 us)
Async XLA Ops:
  7.2 82.1 %copy-start = (bf16[128,4608]{1,0:T(8,128)(2,1)S(1)}, bf16[128,4608]{1,0:T(8,128)(2,1)}, u32[]{:S(2)}) copy-start(bf16[128,4608]{1,0:T(8,128)(2,1)} %param.25) | copy-start | bytes 3538948
  7.2 70.0 %all-gather.10.cloned.1.call-start = ((), (), s32[]{:S(2)}) async-start(), calls=%async_computation.5 | async-start | bytes 4595712 | tf_op jit(solution)/shard_map/all_gather | solution.py:68
  9.7 110.9 %all-gather.12.cloned.1.call-start = ((), (), s32[]{:S(2)}) async-start(), calls=%async_computation.6 | async-start | bytes 5242880 | tf_op jit(solution)/shard_map/all_gather | solution.py:334
  11.2 72.1 %copy-start.54 = (f32[64]{0:T(128)}, f32[64]{0:T(128)S(1)}, u32[]{:S(2)}) copy-start(f32[64]{0:T(128)S(1)} %convert_element_type.304) | copy-start | bytes 772
  12.7 89.2 %copy-start.50 = (f32[512]{0:T(512)}, f32[512]{0:T(512)S(1)}, u32[]{:S(2)}) copy-start(f32[512]{0:T(512)S(1)} %add_rsqrt_fusion.3) | copy-start | bytes 6148
  13.1 93.0 %copy-start.37 = (f32[512,32]{0,1:T(8,128)}, f32[512,32]{0,1:T(8,128)S(1)}, u32[]{:S(2)}) copy-start(f32[512,32]{0,1:T(8,128)S(1)} %get-tuple-element.56) | copy-start | bytes 196612
  13.1 93.0 %copy-start.39 = (f32[512,32]{0,1:T(8,128)}, f32[512,32]{0,1:T(8,128)S(1)}, u32[]{:S(2)}) copy-start(f32[512,32]{0,1:T(8,128)S(1)} %get-tuple-element.57) | copy-start | bytes 196612
  13.1 68.1 %copy-start.18 = (bf16[1,512,1024]{2,1,0:T(8,128)(2,1)S(1)}, bf16[1,512,1024]{2,1,0:T(8,128)(2,1)}, u32[]{:S(2)}) copy-start(bf16[1,512,1024]{2,1,0:T(8,128)(2,1)} %param.14) | copy-start | bytes 3145732
  81.2 20.8 %copy-start.48 = (f32[1024]{0:T(1024)}, f32[1024]{0:T(1024)S(1)}, u32[]{:S(2)}) copy-start(f32[1024]{0:T(1024)S(1)} %get-tuple-element.24) | copy-start | bytes 12292
  87.6 6.5 copy-start.57
  87.6 6.6 copy-start.56
  87.7 93.2 %all-gather.14.cloned.1.call-start = ((), (), s32[]{:S(2)}) async-start(), calls=%async_computation.7 | async-start | bytes 2162688 | tf_op jit(solution)/shard_map/all_gather | solution.py:68
  89.2 175.9 %all-gather.16.cloned.1.call-start = ((), (), s32[]{:S(2)}) async-start(), calls=%async_computation.8 | async-start | bytes 9732096 | tf_op jit(solution)/shard_map/all_gather | solution.py:68
  90.0 259.0 %all-gather.18.cloned.1.call-start = ((), (), s32[]{:S(2)}) async-start(), calls=%async_computation.9 | async-start | bytes 9732096 | tf_op jit(solution)/shard_map/all_gather | solution.py:68
  91.8 341.2 %all-gather.20.cloned.1.call-start = ((), (), s32[]{:S(2)}) async-start(), calls=%async_computation.10 | async-start | bytes 9732096 | tf_op jit(solution)/shard_map/all_gather | solution.py:68
  93.6 699.5 %reduce-scatter.10.cloned.1.call-start = ((), (), s32[]{:S(2)}) async-start(), calls=%async_computation.13 | async-start | bytes 2654208 | tf_op jit(solution)/shard_map/reduce_scatter | solution.py:92
  94.2 10.8 %copy-start.52 = (f32[64]{0:T(128)}, f32[64]{0:T(128)S(1)}, u32[]{:S(2)}) copy-start(f32[64]{0:T(128)S(1)} %convert_element_type.300) | copy-start | bytes 772
  123.1 57.7 %copy-start.19 = (bf16[1,512,1024]{2,1,0:T(8,128)(2,1)S(1)}, bf16[1,512,1024]{2,1,0:T(8,128)(2,1)}, u32[]{:S(2)}) copy-start(bf16[1,512,1024]{2,1,0:T(8,128)(2,1)} %param.14) | copy-start | bytes 3145732
  157.1 390.7 %copy-start.6 = (bf16[512,1024]{1,0:T(8,128)(2,1)}, bf16[512,1024]{1,0:T(8,128)(2,1)S(1)}, u32[]{:S(2)}) copy-start(bf16[512,1024]{1,0:T(8,128)(2,1)S(1)} %get-tuple-element.18) | copy-start | bytes 3145732
  458.8 5.1 copy-start.24
  463.9 13.4 %collective-permute-start.6 = (bf16[8,2,32,4608]{3,2,1,0:T(8,128)(2,1)}, bf16[8,2,32,4608]{3,2,1,0:T(8,128)(2,1)}, u32[]{:S(2)}, u32[]{:S(2)}) collective-permute-start(bf16[8,2,32,4608]{3,2,1,0:T(8,128)(2,1)} %dynamic-slice_bitcast_fusion.2), channel_id=1, source_target_pairs={{0,8},{8,0},{16,24},{24,16},{1,9},{9,1},{17,25},{25,17},{2,10},{10... | collective-permute-start | bytes 14155784 | tf_op jit(solution)/shard_map/ppermute | solution.py:81
  464.1 13.1 %slice-start.4 = ((s8[9437184]{0:T(1024)(128)(4,1)}), s8[4194304]{0:T(1024)(128)(4,1)S(1)}, s32[]{:S(2)}) async-start(s8[9437184]{0:T(1024)(128)(4,1)} %bitcast.171), calls=%async_computation.23 | async-start | bytes 8388608
  464.1 13.1 %slice-start.5 = ((s8[9437184]{0:T(1024)(128)(4,1)}), s8[4194304]{0:T(1024)(128)(4,1)S(1)}, s32[]{:S(2)}) async-start(s8[9437184]{0:T(1024)(128)(4,1)} %bitcast.171), calls=%async_computation.24 | async-start | bytes 8388608
  471.9 5.1 copy-start.25
  471.9 5.3 slice-start.6
  477.0 59.9 %collective-permute-start.8 = (bf16[8,2,32,4608]{3,2,1,0:T(8,128)(2,1)}, bf16[8,2,32,4608]{3,2,1,0:T(8,128)(2,1)}, u32[]{:S(2)}, u32[]{:S(2)}) collective-permute-start(bf16[8,2,32,4608]{3,2,1,0:T(8,128)(2,1)} %dynamic-slice_bitcast_fusion.1), channel_id=1, source_target_pairs={{0,8},{8,0},{16,24},{24,16},{1,9},{9,1},{17,25},{25,17},{2,10},{10... | collective-permute-start | bytes 14155784 | tf_op jit(solution)/shard_map/ppermute | solution.py:81
  481.0 11.1 %slice-start.7 = ((s8[4718592]{0:T(1024)(128)(4,1)}), s8[4194304]{0:T(1024)(128)(4,1)S(1)}, s32[]{:S(2)}) async-start(s8[4718592]{0:T(1024)(128)(4,1)} %bitcast.197), calls=%async_computation.26 | async-start | bytes 8388608
  481.2 10.9 %copy-start.27 = (f32[512,1024]{1,0:T(8,128)S(1)}, f32[512,1024]{1,0:T(8,128)}, u32[]{:S(2)}) copy-start(f32[512,1024]{1,0:T(8,128)} %copy-done.26) | copy-start | bytes 6291460
  481.2 10.9 %slice-start.8 = ((s8[4718592]{0:T(1024)(128)(4,1)}), s8[524288]{0:T(1024)(128)(4,1)S(1)}, s32[]{:S(2)}) async-start(s8[4718592]{0:T(1024)(128)(4,1)} %bitcast.197), calls=%async_computation.27 | async-start | bytes 1048576
  481.2 53.5 %collective-permute-start.7 = (bf16[8,1,32,4608]{3,2,1,0:T(8,128)(2,1)S(1)}, bf16[8,1,32,4608]{3,2,1,0:T(8,128)(2,1)S(1)}, u32[]{:S(2)}, u32[]{:S(2)}) collective-permute-start(bf16[8,1,32,4608]{3,2,1,0:T(8,128)(2,1)S(1)} %constant_dynamic-slice_fusion.2), channel_id=1, source_target_pairs={{0,16},{8,24},{16,0},{24,8},{1,17},{9,25},{17,1},{25,9},{2,18},{10... | collective-permute-start | bytes 7077896 | tf_op jit(solution)/shard_map/ppermute | solution.py:81
  536.8 256.9 %reduce-scatter.12.cloned.1.call-start = ((), (), s32[]{:S(2)}) async-start(), calls=%async_computation.15 | async-start | bytes 2654208 | tf_op jit(solution)/shard_map/reduce_scatter | solution.py:92
  536.9 10.3 %copy-start.41 = (bf16[1,512,1024]{2,1,0:T(8,128)(2,1)S(1)}, bf16[1,512,1024]{2,1,0:T(8,128)(2,1)}, u32[]{:S(2)}) copy-start(bf16[1,512,1024]{2,1,0:T(8,128)(2,1)} %param.15) | copy-start | bytes 3145732
  542.2 3.5 copy-start.12
  542.2 5.0 copy-start.28
  542.2 5.0 copy-start.36
  545.7 52.9 %collective-permute-start.9 = (bf16[8,1,32,4608]{3,2,1,0:T(8,128)(2,1)}, bf16[8,1,32,4608]{3,2,1,0:T(8,128)(2,1)}, u32[]{:S(2)}, u32[]{:S(2)}) collective-permute-start(bf16[8,1,32,4608]{3,2,1,0:T(8,128)(2,1)} %constant_dynamic-slice_fusion.1), channel_id=1, source_target_pairs={{0,16},{8,24},{16,0},{24,8},{1,17},{9,25},{17,1},{25,9},{2,18},{10... | collective-permute-start | bytes 7077896 | tf_op jit(solution)/shard_map/ppermute | solution.py:81
  554.7 44.0 %slice-start.2 = ((s8[4718592]{0:T(1024)(128)(4,1)}), s8[524288]{0:T(1024)(128)(4,1)S(1)}, s32[]{:S(2)}) async-start(s8[4718592]{0:T(1024)(128)(4,1)} %bitcast.161), calls=%async_computation.21 | async-start | bytes 1048576
  556.7 42.0 %slice-start.3 = ((s8[4718592]{0:T(1024)(128)(4,1)}), s8[4194304]{0:T(1024)(128)(4,1)S(1)}, s32[]{:S(2)}) async-start(s8[4718592]{0:T(1024)(128)(4,1)} %bitcast.161), calls=%async_computation.22 | async-start | bytes 8388608
  564.7 5.0 copy-start.23
  569.7 103.4 %collective-permute-start.10 = (bf16[8,2,144,1024]{3,2,1,0:T(8,128)(2,1)}, bf16[8,2,144,1024]{3,2,1,0:T(8,128)(2,1)}, u32[]{:S(2)}, u32[]{:S(2)}) collective-permute-start(bf16[8,2,144,1024]{3,2,1,0:T(8,128)(2,1)} %dynamic-slice_bitcast_fusion), channel_id=1, source_target_pairs={{0,8},{8,0},{16,24},{24,16},{1,9},{9,1},{17,25},{25,17},{2,10},{10... | collective-permute-start | bytes 14155784 | tf_op jit(solution)/shard_map/ppermute | solution.py:81
  602.3 206.6 %reduce-scatter.8.cloned.1.call-start = ((), (), s32[]{:S(2)}) async-start(), calls=%async_computation.12 | async-start | bytes 589824 | tf_op jit(solution)/shard_map/reduce_scatter | solution.py:92
  651.8 3.1 copy-start.16
  651.8 3.1 copy-start.7
  651.9 4.1 copy-start.14
  655.0 13.9 %collective-permute-start = (bf16[1,2,512,1024]{3,2,1,0:T(8,128)(2,1)}, bf16[1,2,512,1024]{3,2,1,0:T(8,128)(2,1)}, u32[]{:S(2)}, u32[]{:S(2)}) collective-permute-start(bf16[1,2,512,1024]{3,2,1,0:T(8,128)(2,1)} %dynamic-slice_bitcast_fusion.4), channel_id=1, source_target_pairs={{0,8},{8,0},{16,24},{24,16},{1,9},{9,1},{17,25},{25,17},{2,10},{10... | collective-permute-start | bytes 6291464 | tf_op jit(solution)/shard_map/ppermute | solution.py:81
  659.6 4.9 collective-permute-start.4
  664.6 4.3 copy-start.17
  667.3 17.9 %collective-permute-start.5 = (bf16[8,1,32,1024]{3,2,1,0:T(8,128)(2,1)S(1)}, bf16[8,1,32,1024]{3,2,1,0:T(8,128)(2,1)S(1)}, u32[]{:S(2)}, u32[]{:S(2)}) collective-permute-start(bf16[8,1,32,1024]{3,2,1,0:T(8,128)(2,1)S(1)} %constant_dynamic-slice_fusion.3), channel_id=1, source_target_pairs={{0,16},{8,24},{16,0},{24,8},{1,17},{9,25},{17,1},{25,9},{2,18},{10... | collective-permute-start | bytes 1572872 | tf_op jit(solution)/shard_map/ppermute | solution.py:81
  672.5 32.2 %collective-permute-start.1 = (bf16[1,1,512,1024]{3,2,1,0:T(8,128)(2,1)}, bf16[1,1,512,1024]{3,2,1,0:T(8,128)(2,1)}, u32[]{:S(2)}, u32[]{:S(2)}) collective-permute-start(bf16[1,1,512,1024]{3,2,1,0:T(8,128)(2,1)} %constant_dynamic-slice_fusion.5), channel_id=1, source_target_pairs={{0,16},{8,24},{16,0},{24,8},{1,17},{9,25},{17,1},{25,9},{2,18},{10... | collective-permute-start | bytes 3145736 | tf_op jit(solution)/shard_map/ppermute | solution.py:81
  682.2 72.7 %collective-permute-start.11 = (bf16[8,1,144,1024]{3,2,1,0:T(8,128)(2,1)}, bf16[8,1,144,1024]{3,2,1,0:T(8,128)(2,1)}, u32[]{:S(2)}, u32[]{:S(2)}) collective-permute-start(bf16[8,1,144,1024]{3,2,1,0:T(8,128)(2,1)} %constant_dynamic-slice_fusion), channel_id=1, source_target_pairs={{0,16},{8,24},{16,0},{24,8},{1,17},{9,25},{17,1},{25,9},{2,18},{10... | collective-permute-start | bytes 7077896 | tf_op jit(solution)/shard_map/ppermute | solution.py:81
  686.3 140.7 %reduce-scatter.14.cloned.1.call-start = ((), (), s32[]{:S(2)}) async-start(), calls=%async_computation.17 | async-start | bytes 2654208 | tf_op jit(solution)/shard_map/reduce_scatter | solution.py:92
  710.6 44.3 %slice-start = ((s8[4718592]{0:T(1024)(128)(4,1)}), s8[4194304]{0:T(1024)(128)(4,1)S(1)}, s32[]{:S(2)}) async-start(s8[4718592]{0:T(1024)(128)(4,1)} %bitcast.159), calls=%async_computation.19 | async-start | bytes 8388608
  710.9 5.6 copy-start.34
  711.8 43.1 %slice-start.1 = ((s8[4718592]{0:T(1024)(128)(4,1)}), s8[524288]{0:T(1024)(128)(4,1)S(1)}, s32[]{:S(2)}) async-start(s8[4718592]{0:T(1024)(128)(4,1)} %bitcast.159), calls=%async_computation.20 | async-start | bytes 1048576
  759.1 134.3 %reduce-scatter.6.cloned.1.call-start = ((), (), s32[]{:S(2)}) async-start(), calls=%async_computation.11 | async-start | bytes 1179648 | tf_op jit(solution)/shard_map/reduce_scatter | solution.py:92
  759.2 6.1 copy-start.31
  761.1 4.2 collective-permute-start.2
  766.3 25.3 %collective-permute-start.3 = (bf16[8,1,32,2048]{3,2,1,0:T(8,128)(2,1)S(1)}, bf16[8,1,32,2048]{3,2,1,0:T(8,128)(2,1)S(1)}, u32[]{:S(2)}, u32[]{:S(2)}) collective-permute-start(bf16[8,1,32,2048]{3,2,1,0:T(8,128)(2,1)S(1)} %constant_dynamic-slice_fusion.4), channel_id=1, source_target_pairs={{0,16},{8,24},{16,0},{24,8},{1,17},{9,25},{17,1},{25,9},{2,18},{10... | collective-permute-start | bytes 3145736 | tf_op jit(solution)/shard_map/ppermute | solution.py:81
  793.1 118.3 %all-gather.22.cloned.1.call-start = ((), (), s32[]{:S(2)}) async-start(), calls=%async_computation.14 | async-start | bytes 1474560 | tf_op jit(solution)/shard_map/all_gather | solution.py:95
  793.6 136.7 %all-gather.24.cloned.1.call-start = ((), (), s32[]{:S(2)}) async-start(), calls=%async_computation.16 | async-start | bytes 1474560 | tf_op jit(solution)/shard_map/all_gather | solution.py:95
  794.4 4.7 copy-start.29
  794.4 154.9 %all-gather.26.cloned.1.call-start = ((), (), s32[]{:S(2)}) async-start(), calls=%async_computation.18 | async-start | bytes 1474560 | tf_op jit(solution)/shard_map/all_gather | solution.py:95
  827.0 46.5 %copy-start.15 = (f32[512,1024]{1,0:T(8,128)S(1)}, f32[512,1024]{1,0:T(8,128)}, u32[]{:S(2)}) copy-start(f32[512,1024]{1,0:T(8,128)} %copy-done.13) | copy-start | bytes 6291460
  930.4 21.9 %copy-start.1 = (bf16[128,4608]{1,0:T(8,128)(2,1)S(1)}, bf16[128,4608]{1,0:T(8,128)(2,1)}, u32[]{:S(2)}) copy-start(bf16[128,4608]{1,0:T(8,128)(2,1)} %param.25) | copy-start | bytes 3538948
  (29 other events, 49.6 us)
Sparse Core Ops, SparseCore 0:
  11.5 65.6 all-gather.9
  87.8 32.8 all-gather.11
  124.1 56.7 all-gather.13
  184.1 80.8 all-gather.15
  268.4 80.6 all-gather.17
  352.4 80.6 all-gather.19
  536.9 67.7 reduce-scatter.9
  608.7 67.8 reduce-scatter.11
  686.4 60.6 reduce-scatter.7
  759.2 67.7 reduce-scatter.13
  830.8 62.5 reduce-scatter.5
  894.8 16.4 all-gather.21
  912.9 17.4 all-gather.23
  931.8 17.4 all-gather.25

commit v2 on v1

--- a/solution.py
+++ b/solution.py
@@ -68,9 +68,9 @@
     return lax.all_gather(own, ("fsdp", "ctx"), axis=0, tiled=True)
 
 
-def halve_over_ctx(parts):
-    count = lax.axis_size("ctx")
-    me = lax.axis_index("ctx")
+def halve_over(axis, parts):
+    count = lax.axis_size(axis)
+    me = lax.axis_index(axis)
     step = 1
     while step < count:
         lead, left, rows, width = parts.shape
@@ -78,21 +78,59 @@
         bit = (me // step) % 2
         keep = lax.dynamic_index_in_dim(pairs, bit, 2, keepdims=False)
         send = lax.dynamic_index_in_dim(pairs, 1 - bit, 2, keepdims=False)
-        got = lax.ppermute(send, "ctx", [(i, i ^ step) for i in range(count)])
+        got = lax.ppermute(send, axis, [(i, i ^ step) for i in range(count)])
         parts = (keep.astype(jnp.float32) + got.astype(jnp.float32)).astype(jnp.bfloat16)
         step *= 2
     return parts[:, 0]
 
 
-def scatter_rows(grad):
+def double_over_ctx(part):
+    count = lax.axis_size("ctx")
+    me = lax.axis_index("ctx")
+    rows, width = part.shape
+    held = part[None]
+    step = count // 2
+    while step >= 1:
+        got = lax.ppermute(held, "ctx", [(i, i ^ step) for i in range(count)])
+        upper = (me // step) % 2 == 1
+        held = jnp.stack(
+            [jnp.where(upper, got, held), jnp.where(upper, held, got)], axis=1
+        ).reshape(2 * held.shape[0], rows, width)
+        step //= 2
+    return held
+
+
+def gather_rows_split(shard):
+    owners, count = lax.axis_size("fsdp"), lax.axis_size("ctx")
+    part = shard.shape[0] // count
+    own = lax.dynamic_slice_in_dim(shard, lax.axis_index("ctx") * part, part, 0)
+    held = double_over_ctx(lax.all_gather(own, "fsdp", axis=0, tiled=True))
+    held = held.reshape(count, owners, part, shard.shape[1])
+    return held.transpose(1, 0, 2, 3).reshape(owners * count * part, shard.shape[1])
+
+
+def scatter_rows(grad, by_permutes):
     owners, count = lax.axis_size("fsdp"), lax.axis_size("ctx")
     rows, width = grad.shape
     part = rows // (owners * count)
-    mine = halve_over_ctx(grad.reshape(owners, count, part, width))
-    mine = lax.psum_scatter(
-        mine.reshape(owners * part, width), "fsdp", scatter_dimension=0, tiled=True
-    )
-    return lax.all_gather(mine, "ctx", axis=0, tiled=True).astype(jnp.float32)
+    mine = halve_over("ctx", grad.reshape(owners, count, part, width))
+    if by_permutes:
+        mine = halve_over("fsdp", mine[None])[0]
+    else:
+        mine = lax.psum_scatter(
+            mine.reshape(owners * part, width), "fsdp", scatter_dimension=0, tiled=True
+        )
+    return double_over_ctx(mine).reshape(count * part, width).astype(jnp.float32)
+
+
+def sum_everywhere(terms):
+    for axis in ("ctx", "fsdp"):
+        count = lax.axis_size(axis)
+        step = 1
+        while step < count:
+            terms = terms + lax.ppermute(terms, axis, [(i, i ^ step) for i in range(count)])
+            step *= 2
+    return terms
 
 
 def place(values, side):
@@ -288,8 +326,8 @@
     gain_ffn_low = w_first[:, width_q + 2 * width_k + 1]
     w_out = gather_rows(out_weight)
     w_gate, w_up, w_down = (
-        gather_rows(gate_weight),
-        gather_rows(up_weight),
+        gather_rows_split(gate_weight),
+        gather_rows_split(up_weight),
         gather_rows(down_weight),
     )
     gain_attn = gain_attn_low.astype(jnp.float32)
@@ -331,9 +369,8 @@
     keys_low = (
         rotate(k_normed, cosine, sine).reshape(tokens, kv_count * head_width).astype(jnp.bfloat16)
     )
-    key_value = lax.all_gather(
-        jnp.concatenate([keys_low, values_low], axis=1), "ctx", axis=0, tiled=True
-    )
+    key_value = double_over_ctx(jnp.concatenate([keys_low, values_low], axis=1))
+    key_value = key_value.reshape(-1, 2 * width_k)
     key_all, value_all = key_value[:, :width_k], key_value[:, width_k:]
     mixed, inverse_sums = attend(places, queries, key_all, value_all)
     resid = hidden_in + jnp.dot(mixed, w_out, preferred_element_type=jnp.float32)
@@ -372,10 +409,11 @@
     grad_queries, grad_keys_all, grad_values_all = attend_back(
         places, queries, key_all, value_all, grad_mixed, inverse_sums, delta
     )
-    grad_own = halve_over_ctx(
+    grad_own = halve_over(
+        "ctx",
         jnp.concatenate([grad_keys_all, grad_values_all], axis=1).reshape(
             1, lax.axis_size("ctx"), tokens, 2 * width_k
-        )
+        ),
     )[0].astype(jnp.float32)
     grad_keys_own, grad_values_own = grad_own[:, :width_k], grad_own[:, width_k:]
     grad_q_normed = unrotate(grad_queries.reshape(tokens, heads_count, head_width), cosine, sine)
@@ -397,11 +435,17 @@
     input_grad = (grad_resid + grad_input_norm).astype(jnp.bfloat16)
     attn_gain_sum = jnp.sum(attn_gain_terms, axis=0)
     down_owned, gate_owned, up_owned, out_owned, first_owned = (
-        scatter_rows(grad.astype(jnp.bfloat16))
-        for grad in (down_grad, gate_grad, up_grad, out_grad, first_grad)
+        scatter_rows(grad.astype(jnp.bfloat16), by_permutes)
+        for grad, by_permutes in (
+            (down_grad, False),
+            (gate_grad, True),
+            (up_grad, False),
+            (out_grad, True),
+            (first_grad, True),
+        )
     )
     width = attn_gain_sum.shape[0]
-    gain_sums = lax.psum(
+    gain_sums = sum_everywhere(
         jnp.concatenate(
             [
                 attn_gain_sum,
@@ -409,8 +453,7 @@
                 jnp.sum(query_gain_terms, axis=(0, 1)),
                 jnp.sum(key_gain_terms, axis=(0, 1)),
             ]
-        ),
-        ("ctx", "fsdp"),
+        )
     )
     own_gain = lax.axis_index("fsdp") * attn_gain.shape[0]
     attn_owned = lax.dynamic_slice_in_dim(gain_sums, own_gain, attn_gain.shape[0])

time: 964 us -> 905 us (0.939)
  waiting for transfers between devices: 541 us -> 439 us
  blocking collectives: 53.3 us -> 0 us
  local copies, waits for them, and re-layouts: 73.3 us -> 118 us
  other arithmetic: 67 us -> 104 us
  starting transfers between devices: 9.74 us -> 30.2 us
  matrix products: 124 us -> 113 us
    all_gather x5 -> x3, waiting for transfers between devices: 313 us -> 1.23 us  [gather_rows(): return lax.all_gather(own, ('fsdp', 'ctx'), axis=0, tiled=True)]
    ppermute x12 -> x42, waiting for transfers between devices: 147 us -> 297 us  [the longest x21 196 us: halve_over(): got = lax.ppermute(send, axis, [(i, i ^ step) for i in range(count)])]
    all_gather x4 -> x2, waiting for transfers between devices: 54.3 us -> 103 us  [gather_rows_split(): held = double_over_ctx(lax.all_gather(own, 'fsdp', axis=0, tiled=True))]
    another operation x2 -> x24, other arithmetic: 0.52 us -> 42.2 us  [the longest x19 41.5 us: double_over_ctx(): jnp.stack([jnp.where(upper, got, held), jnp.where(upper, held, got)], axi...]
    psum x1 -> x0, blocking collectives: 40 us -> none  [body(): lax.psum(jnp.concatenate([attn_gain_sum, ffn_gain_sum, jnp.sum(query_gain...]
    ppermute x12 -> x42, starting transfers between devices: 8.53 us -> 29.7 us  [the longest x21 21.1 us: halve_over(): got = lax.ppermute(send, axis, [(i, i ^ step) for i in range(count)])]
    dynamic_slice x0 -> x8, local copies, waits for them, and re-layouts: none -> 18.1 us  [the longest x3 9.02 us: halve_over(): keep = lax.dynamic_index_in_dim(pairs, bit, 2, keepdims=False)]
    transpose x0 -> x2, local copies, waits for them, and re-layouts: none -> 17.4 us  [gather_rows_split(): held.transpose(1, 0, 2, 3).reshape(owners * count * part, shard.shape[1])]
  transfers between devices with their start and end apart: 26 -> 49, of which waited for: 17 -> 20; matrix products, arithmetic and copies ran while one was open for 20% -> 29% of each run, Pallas kernels for 8% -> 3%
where the time goes in v2:
time: 905 us; the launch traced here: 896 us
  waiting for transfers between devices  439 us (49%)
  local copies, waits for them, and re-layouts  118 us (13%)
  matrix products  113 us (12%)
  other arithmetic  104 us (11%)
  Pallas kernels  75.1 us (8%)
  starting transfers between devices  30.2 us (3%)
  between operations  16.2 us (2%)
    ppermute x21, waiting for transfers between devices, halve_over(): got = lax.ppermute(send, axis, [(i, i ^ step) for i in range(count)])  196 us
    all_gather x2, waiting for transfers between devices, gather_rows_split(): held = double_over_ctx(lax.all_gather(own, 'fsdp', axis=0, tiled=True))  103 us
    ppermute x16, waiting for transfers between devices, double_over_ctx(): got = lax.ppermute(held, 'ctx', [(i, i ^ step) for i in range(count)])  96.4 us
    dot_general x7, matrix products, times_transposed(): lax.dot_general(left, right, (((1,), (1,)), ((), ())), preferred_element_...  49.7 us
    pallas_call x1, Pallas kernels, attend_back(): pl.pallas_call(backward_kernel, grid_spec=pltpu.PrefetchScalarGridSpec(nu...  43.8 us
    another operation x19, other arithmetic, double_over_ctx(): jnp.stack([jnp.where(upper, got, held), jnp.where(upper, held, got)], axi...  41.5 us
    reduce_scatter x2, waiting for transfers between devices, scatter_rows(): lax.psum_scatter(mine.reshape(owners * part, width), 'fsdp', scatter_dime...  38.7 us
    convert_element_type x17, other arithmetic, halve_over(): (keep.astype(jnp.float32) + got.astype(jnp.float32)).astype(jnp.bfloat16)  34.4 us
  transfers between devices with their start and end apart: 49, of which 20 were waited for; matrix products, arithmetic and copies ran while one was open for 29% of the time, Pallas kernels for 3%

profile of v2, /device:TPU:0, one launch (start us, length us, event | category | flops | bytes accessed | tf_op | source)
XLA Modules:
  0.0 895.8 jit_solution(12989261468569205977)
XLA Ops:
  15.0 50.6 %all-gather.12.cloned.1.call-done = bf16[256,4608]{1,0:T(8,128)(2,1)} async-done(((bf16[32,4608]{1,0:T(8,128)(2,1)}), bf16[256,4608]{1,0:T(8,128)(2,1)}) %all-gather.12.cloned.1.call-update) | async-done | bytes 2359312 | tf_op jit(solution)/shard_map/all_gather | solution.py:107
  67.1 51.9 %all-gather.10.cloned.1.call-done = bf16[256,4608]{1,0:T(8,128)(2,1)} async-done(((bf16[32,4608]{1,0:T(8,128)(2,1)}), bf16[256,4608]{1,0:T(8,128)(2,1)}) %all-gather.10.cloned.1.call-update) | async-done | bytes 2359312 | tf_op jit(solution)/shard_map/all_gather | solution.py:107
  124.2 59.8 %collective-permute-done.2 = bf16[1,256,4608]{2,1,0:T(8,128)(2,1)} collective-permute-done((bf16[1,256,4608]{2,1,0:T(8,128)(2,1)}, bf16[1,256,4608]{2,1,0:T(8,128)(2,1)}, u32[]{:S(2)}, u32[]{:S(2)}) %collective-permute-start.2) | collective-permute-done | bytes 2359328 | tf_op jit(solution)/shard_map/ppermute | solution.py:94
  184.0 4.2 select_bitcast_fusion.5
  188.2 2.8 maximum_bitcast_fusion
  192.6 2.5 maximum_bitcast_fusion.1
  196.3 3.1 slice_bitcast_fusion
  199.4 3.9 copy.85
  203.4 2.4 slice_bitcast_fusion.1
  205.7 2.3 copy.86
  213.0 2.3 convolution_convert_fusion.6
  221.9 25.3 %collective-permute-done = bf16[1,512,1024]{1,2,0:T(8,128)(2,1)} collective-permute-done((bf16[1,512,1024]{1,2,0:T(8,128)(2,1)}, bf16[1,512,1024]{1,2,0:T(8,128)(2,1)}, u32[]{:S(2)}, u32[]{:S(2)}) %collective-permute-start) | collective-permute-done | bytes 1048608 | tf_op jit(solution)/shard_map/ppermute | solution.py:94
  252.5 6.2 select_bitcast_fusion.3
  258.7 8.3 pad_maximum_fusion
  267.1 8.2 copy.90
  275.2 7.5 select_bitcast_fusion.1
  282.7 8.6 pad_maximum_fusion.1
  291.3 7.9 copy.91
  299.2 9.2 %copy.92 = bf16[8,4,32,4608]{3,2,1,0:T(8,128)(2,1)} copy(bf16[8,4,32,4608]{3,2,0,1:T(8,128)(2,1)} %bitcast.358) | data formatting | bytes 18874368 | tf_op jit(solution)/shard_map/transpose | solution.py:109
  310.3 2.3 pad_maximum_fusion.2
  312.6 6.3 copy.87
  318.9 2.5 fusion.71
  321.5 31.2 %attention_forward.1 = (bf16[512,1024]{1,0:T(8,128)(2,1)S(1)}, f32[4,4,512]{2,1,0:T(4,128)S(1)}) custom-call(s32[10]{0:T(128)S(1)} %pad_add_fusion.place_ref, bf16[512,1024]{1,0:T(8,128)(2,1)S(1)} %copy.88.q_ref, bf16[2048,512]{1,0:T(8,128)(2,1)S(1)} %get-tuple-element.51.k_ref, bf16[2048,512]{1,0:T(8,128)(2,1)S(1)} %get-tuple-element.50.v_ref), custom_call_target="tpu_custom_call" | custom-call | flops 6442450944 | bytes 12582912 | tf_op jit(solution)/shard_map/attention_forward/pallas_call | solution.py:254
  355.4 2.9 multiply_reduce_fusion.4
  359.9 11.6 %fusion.76 = f32[512,4608]{1,0:T(8,128)} fusion(bf16[512,1024]{1,0:T(8,128)(2,1)S(1)} %multiply_convert_fusion.2, bf16[1024,4608]{1,0:T(8,128)(2,1)} %bitcast.368), kind=kOutput, calls=%fused_computation.250 | convolution fusion | flops 4831838208 | bytes 19922944 | tf_op jit(solution)/shard_map/dot_general | solution.py:380
  371.5 7.4 fusion.77
  378.9 18.4 %fusion.6 = (bf16[512,4608]{1,0:T(8,128)(2,1)}, bf16[512,4608]{1,0:T(8,128)(2,1)}, bf16[512,4608]{1,0:T(8,128)(2,1)}) fusion(f32[512,4608]{1,0:T(8,128)} %fusion.76, f32[512,4608]{1,0:T(8,128)} %fusion.77, bf16[4608,1024]{1,0:T(8,128)(2,1)} %all-gather.14.cloned.1.call-done, bf16[1,512,1024]{2,1,0:T(8,128)(2,1)} %param.15), kind=kOutput, calls=%fused_computation.16 | convolution fusion | flops 4867227648 | bytes 43515904 | tf_op jit(solution)/shard_map/dot_general | solution.py:60
  397.4 9.2 %fusion.78 = f32[512,1024]{1,0:T(8,128)S(1)} fusion(bf16[512,4608]{1,0:T(8,128)(2,1)} %get-tuple-element.36, bf16[1024,4608]{1,0:T(8,128)(2,1)} %bitcast.369), kind=kOutput, calls=%fused_computation.252 | convolution fusion | flops 4831838208 | bytes 16252928 | tf_op jit(solution)/shard_map/dot_general | solution.py:60
  406.6 7.5 convolution_convert_fusion.1
  414.1 8.8 multiply_reduce_fusion.1
  423.5 2.7 convolution_convert_fusion.4
  426.2 3.0 convert_multiply_fusion.1
  435.9 43.8 %attention_backward.1 = (f32[512,1024]{1,0:T(8,128)S(1)}, bf16[2048,512]{1,0:T(8,128)(2,1)S(1)}, bf16[2048,512]{1,0:T(8,128)(2,1)S(1)}) custom-call(s32[10]{0:T(128)S(1)} %pad_add_fusion.place_ref, bf16[512,1024]{1,0:T(8,128)(2,1)S(1)} %copy.88.q_ref, bf16[2048,512]{1,0:T(8,128)(2,1)S(1)} %copy-done.5, bf16[2048,512]{1,0:T(8,128)(2,1)S(1)} %copy-done.3, ...), custom_call_target="tpu_custom_call" | custom-call | flops 16106127360 | bytes 16777216 | tf_op jit(solution)/shard_map/attention_backward/pallas_call | solution.py:279
  484.0 5.6 dynamic-slice_bitcast_fusion.1
  489.6 7.8 convolution_convert_fusion
  497.5 6.0 fusion.36
  503.5 7.6 convolution_convert_fusion.2
  513.7 8.3 constant_dynamic-slice_fusion.5
  526.1 5.0 copy.128
  536.0 5.5 collective-permute-done.22
  543.1 3.6 collective-permute-done.23
  546.8 2.6 collective-permute-start.24
  549.3 5.4 dynamic-slice_bitcast_fusion
  554.9 2.6 fusion.9
  560.4 4.5 fusion.34
  564.9 18.3 %collective-permute-done.7 = bf16[1,1,512,1024]{3,2,1,0:T(8,128)(2,1)S(1)} collective-permute-done((bf16[1,1,512,1024]{3,2,1,0:T(8,128)(2,1)S(1)}, bf16[1,1,512,1024]{3,2,1,0:T(8,128)(2,1)S(1)}, u32[]{:S(2)}, u32[]{:S(2)}) %collective-permute-start.7) | collective-permute-done | bytes 1048608 | tf_op jit(solution)/shard_map/ppermute | solution.py:81
  590.5 3.7 fusion.24
  597.9 3.9 convolution_convert_fusion.3
  602.8 2.8 collective-permute-done.10
  609.8 5.5 fusion.1
  618.2 3.7 fusion.2
  621.9 4.0 fusion.8
  632.5 61.3 %collective-permute-done.14 = bf16[8,1,32,2048]{3,2,0,1:T(8,128)(2,1)S(1)} collective-permute-done((bf16[8,1,32,2048]{3,2,0,1:T(8,128)(2,1)S(1)}, bf16[8,1,32,2048]{3,2,0,1:T(8,128)(2,1)S(1)}, u32[]{:S(2)}, u32[]{:S(2)}) %collective-permute-start.14) | collective-permute-done | bytes 1048608 | tf_op jit(solution)/shard_map/ppermute | solution.py:81
  696.4 3.7 add_convert_fusion.1
  700.4 42.2 %collective-permute-done.28 = bf16[8,1,32,4608]{3,2,0,1:T(8,128)(2,1)S(1)} collective-permute-done((bf16[8,1,32,4608]{3,2,0,1:T(8,128)(2,1)}, bf16[8,1,32,4608]{3,2,0,1:T(8,128)(2,1)S(1)}, u32[]{:S(2)}, u32[]{:S(2)}) %collective-permute-start.28) | collective-permute-done | bytes 2359328 | tf_op jit(solution)/shard_map/ppermute | solution.py:81
  745.5 6.2 fusion
  755.5 19.0 %collective-permute-done.29 = bf16[1,4,32,4608]{3,2,1,0:T(8,128)(2,1)S(1)} collective-permute-done((bf16[1,4,32,4608]{3,2,1,0:T(8,128)(2,1)S(1)}, bf16[1,4,32,4608]{3,2,1,0:T(8,128)(2,1)S(1)}, u32[]{:S(2)}, u32[]{:S(2)}) %collective-permute-start.29) | collective-permute-done | bytes 1179680 | tf_op jit(solution)/shard_map/ppermute | solution.py:81
  776.2 2.6 collective-permute-start.17
  778.8 24.5 %collective-permute-done.39 = bf16[8,1,144,1024]{3,2,1,0:T(8,128)(2,1)S(1)} collective-permute-done((bf16[8,1,144,1024]{3,2,1,0:T(8,128)(2,1)S(1)}, bf16[8,1,144,1024]{3,2,1,0:T(8,128)(2,1)S(1)}, u32[]{:S(2)}, u32[]{:S(2)}) %collective-permute-start.39) | collective-permute-done | bytes 2359328 | tf_op jit(solution)/shard_map/ppermute | solution.py:81
  803.3 2.5 add_convert_fusion
  807.6 21.1 %collective-permute-done.31 = bf16[1,1,32,4608]{3,2,1,0:T(8,128)(2,1)S(1)} collective-permute-done((bf16[1,1,32,4608]{3,2,1,0:T(8,128)(2,1)S(1)}, bf16[1,1,32,4608]{3,2,1,0:T(8,128)(2,1)S(1)}, u32[]{:S(2)}, u32[]{:S(2)}) %collective-permute-start.31) | collective-permute-done | bytes 294944 | tf_op jit(solution)/shard_map/ppermute | solution.py:81
  829.1 6.6 collective-permute-done.32
  837.9 38.7 %reduce-scatter.5.cloned.1.call-done = bf16[144,1024]{1,0:T(8,128)(2,1)} async-done(((bf16[1152,1024]{1,0:T(8,128)(2,1)}), bf16[144,1024]{1,0:T(8,128)(2,1)}) %reduce-scatter.5.cloned.1.call-update) | async-done | bytes 294928 | tf_op jit(solution)/shard_map/reduce_scatter | solution.py:120
  880.0 4.5 collective-permute-done.40
  (386 shorter events, 115.5 us)
Async XLA Ops:
  7.2 115.2 %copy-start.69 = (bf16[64]{0:T(256)(128)(2,1)S(1)}, bf16[64]{0:T(256)(128)(2,1)}, u32[]{:S(2)}) copy-start(bf16[64]{0:T(256)(128)(2,1)} %param.21) | copy-start | bytes 388
  7.2 115.3 %copy-start.68 = (s32[1,8]{1,0:T(1,128)S(1)}, s32[1,8]{1,0:T(1,128)}, u32[]{:S(2)}) copy-start(s32[1,8]{1,0:T(1,128)} %param.16) | copy-start | bytes 100
  7.2 115.4 %copy-start.70 = (bf16[64]{0:T(256)(128)(2,1)S(1)}, bf16[64]{0:T(256)(128)(2,1)}, u32[]{:S(2)}) copy-start(bf16[64]{0:T(256)(128)(2,1)} %param.22) | copy-start | bytes 388
  7.2 115.7 %copy-start.23 = (bf16[1,512,1024]{2,1,0:T(8,128)(2,1)S(1)}, bf16[1,512,1024]{2,1,0:T(8,128)(2,1)}, u32[]{:S(2)}) copy-start(bf16[1,512,1024]{2,1,0:T(8,128)(2,1)} %param.14) | copy-start | bytes 3145732
  7.2 58.4 %all-gather.12.cloned.1.call-start = ((), (), s32[]{:S(2)}) async-start(), calls=%async_computation.5 | async-start | bytes 2654208 | tf_op jit(solution)/shard_map/all_gather | solution.py:107
  9.2 109.8 %all-gather.10.cloned.1.call-start = ((), (), s32[]{:S(2)}) async-start(), calls=%async_computation.4 | async-start | bytes 2654208 | tf_op jit(solution)/shard_map/all_gather | solution.py:107
  11.0 185.3 %all-gather.6.cloned.1.call-start = ((), (), s32[]{:S(2)}) async-start(), calls=%async_computation.2 | async-start | bytes 4595712 | tf_op jit(solution)/shard_map/all_gather | solution.py:68
  13.4 342.0 %all-gather.8.cloned.1.call-start = ((), (), s32[]{:S(2)}) async-start(), calls=%async_computation.3 | async-start | bytes 2162688 | tf_op jit(solution)/shard_map/all_gather | solution.py:68
  15.0 364.0 %all-gather.14.cloned.1.call-start = ((), (), s32[]{:S(2)}) async-start(), calls=%async_computation.6 | async-start | bytes 9732096 | tf_op jit(solution)/shard_map/all_gather | solution.py:68
  65.6 58.5 %collective-permute-start.4 = (bf16[1,256,4608]{2,1,0:T(8,128)(2,1)}, bf16[1,256,4608]{2,1,0:T(8,128)(2,1)}, u32[]{:S(2)}, u32[]{:S(2)}) collective-permute-start(bf16[1,256,4608]{2,1,0:T(8,128)(2,1)} %bitcast.393), channel_id=1, source_target_pairs={{0,16},{8,24},{16,0},{24,8},{1,17},{9,25},{17,1},{25,9},{2,18},{10... | collective-permute-start | bytes 7077896 | tf_op jit(solution)/shard_map/ppermute | solution.py:94
  119.0 65.0 %collective-permute-start.2 = (bf16[1,256,4608]{2,1,0:T(8,128)(2,1)}, bf16[1,256,4608]{2,1,0:T(8,128)(2,1)}, u32[]{:S(2)}, u32[]{:S(2)}) collective-permute-start(bf16[1,256,4608]{2,1,0:T(8,128)(2,1)} %bitcast.394), channel_id=1, source_target_pairs={{0,16},{8,24},{16,0},{24,8},{1,17},{9,25},{17,1},{25,9},{2,18},{10... | collective-permute-start | bytes 7077896 | tf_op jit(solution)/shard_map/ppermute | solution.py:94
  122.3 715.5 %reduce-scatter.3.cloned.1.call-start = ((), (), s32[]{:S(2)}) async-start(), calls=%async_computation.7 | async-start | bytes 2654208 | tf_op jit(solution)/shard_map/reduce_scatter | solution.py:120
  122.4 95.6 %copy-start.62 = (f32[64]{0:T(128)}, f32[64]{0:T(128)S(1)}, u32[]{:S(2)}) copy-start(f32[64]{0:T(128)S(1)} %convert_element_type.468) | copy-start | bytes 772
  122.6 88.9 %copy-start.64 = (f32[64]{0:T(128)}, f32[64]{0:T(128)S(1)}, u32[]{:S(2)}) copy-start(f32[64]{0:T(128)S(1)} %convert_element_type.472) | copy-start | bytes 772
  123.2 93.4 %copy-start.60 = (f32[512]{0:T(512)}, f32[512]{0:T(512)S(1)}, u32[]{:S(2)}) copy-start(f32[512]{0:T(512)S(1)} %add_rsqrt_fusion.3) | copy-start | bytes 6148
  124.2 94.4 %copy-start.42 = (f32[512,32]{0,1:T(8,128)}, f32[512,32]{0,1:T(8,128)S(1)}, u32[]{:S(2)}) copy-start(f32[512,32]{0,1:T(8,128)S(1)} %get-tuple-element.94) | copy-start | bytes 196612
  191.8 60.0 %collective-permute-start.3 = (bf16[2,256,4608]{2,1,0:T(8,128)(2,1)}, bf16[2,256,4608]{2,1,0:T(8,128)(2,1)}, u32[]{:S(2)}, u32[]{:S(2)}) collective-permute-start(bf16[2,256,4608]{2,1,0:T(8,128)(2,1)} %maximum_bitcast_fusion), channel_id=1, source_target_pairs={{0,8},{8,0},{16,24},{24,16},{1,9},{9,1},{17,25},{25,17},{2,10},{10... | collective-permute-start | bytes 14155784 | tf_op jit(solution)/shard_map/ppermute | solution.py:94
  195.1 80.2 %collective-permute-start.5 = (bf16[2,256,4608]{2,1,0:T(8,128)(2,1)}, bf16[2,256,4608]{2,1,0:T(8,128)(2,1)}, u32[]{:S(2)}, u32[]{:S(2)}) collective-permute-start(bf16[2,256,4608]{2,1,0:T(8,128)(2,1)} %maximum_bitcast_fusion.1), channel_id=1, source_target_pairs={{0,8},{8,0},{16,24},{24,16},{1,9},{9,1},{17,25},{25,17},{2,10},{10... | collective-permute-start | bytes 14155784 | tf_op jit(solution)/shard_map/ppermute | solution.py:94
  216.4 30.8 %collective-permute-start = (bf16[1,512,1024]{1,2,0:T(8,128)(2,1)}, bf16[1,512,1024]{1,2,0:T(8,128)(2,1)}, u32[]{:S(2)}, u32[]{:S(2)}) collective-permute-start(bf16[1,512,1024]{1,2,0:T(8,128)(2,1)} %maximum_bitcast_fusion.3), channel_id=1, source_target_pairs={{0,16},{8,24},{16,0},{24,8},{1,17},{9,25},{17,1},{25,9},{2,18},{10... | collective-permute-start | bytes 3145736 | tf_op jit(solution)/shard_map/ppermute | solution.py:94
  251.8 56.6 %collective-permute-start.1 = (bf16[2,512,1024]{1,2,0:T(8,128)(2,1)}, bf16[2,512,1024]{1,2,0:T(8,128)(2,1)}, u32[]{:S(2)}, u32[]{:S(2)}) collective-permute-start(bf16[2,512,1024]{1,2,0:T(8,128)(2,1)} %maximum_bitcast_fusion.2), channel_id=1, source_target_pairs={{0,8},{8,0},{16,24},{24,16},{1,9},{9,1},{17,25},{25,17},{2,10},{10... | collective-permute-start | bytes 6291464 | tf_op jit(solution)/shard_map/ppermute | solution.py:94
  321.4 33.9 %copy-start.25 = (bf16[1,512,1024]{2,1,0:T(8,128)(2,1)S(1)}, bf16[1,512,1024]{2,1,0:T(8,128)(2,1)}, u32[]{:S(2)}) copy-start(bf16[1,512,1024]{2,1,0:T(8,128)(2,1)} %param.14) | copy-start | bytes 3145732
  359.6 11.8 %slice-start.2 = ((s8[9437184]{0:T(1024)(128)(4,1)}), s8[4194304]{0:T(1024)(128)(4,1)S(1)}, s32[]{:S(2)}) async-start(s8[9437184]{0:T(1024)(128)(4,1)} %bitcast.371), calls=%async_computation.11 | async-start | bytes 8388608
  359.9 46.7 %copy-start.46 = (bf16[512,1024]{1,0:T(8,128)(2,1)}, bf16[512,1024]{1,0:T(8,128)(2,1)S(1)}, u32[]{:S(2)}) copy-start(bf16[512,1024]{1,0:T(8,128)(2,1)S(1)} %multiply_convert_fusion.2) | copy-start | bytes 3145732
  359.9 11.6 %slice-start.3 = ((s8[9437184]{0:T(1024)(128)(4,1)}), s8[4194304]{0:T(1024)(128)(4,1)S(1)}, s32[]{:S(2)}) async-start(s8[9437184]{0:T(1024)(128)(4,1)} %bitcast.371), calls=%async_computation.12 | async-start | bytes 8388608
  481.9 73.0 %collective-permute-start.6 = (bf16[1,2,512,1024]{3,2,1,0:T(8,128)(2,1)}, bf16[1,2,512,1024]{3,2,1,0:T(8,128)(2,1)}, u32[]{:S(2)}, u32[]{:S(2)}) collective-permute-start(bf16[1,2,512,1024]{3,2,1,0:T(8,128)(2,1)} %dynamic-slice_bitcast_fusion.2), channel_id=1, source_target_pairs={{0,8},{8,0},{16,24},{24,16},{1,9},{9,1},{17,25},{25,17},{2,10},{10... | collective-permute-start | bytes 6291464 | tf_op jit(solution)/shard_map/ppermute | solution.py:81
  483.8 27.3 %collective-permute-start.20 = (bf16[8,2,32,1024]{3,2,0,1:T(8,128)(2,1)S(1)}, bf16[8,2,32,1024]{3,2,0,1:T(8,128)(2,1)S(1)}, u32[]{:S(2)}, u32[]{:S(2)}) collective-permute-start(bf16[8,2,32,1024]{3,2,0,1:T(8,128)(2,1)S(1)} %bitcast.403), channel_id=1, source_target_pairs={{0,8},{8,0},{16,24},{24,16},{1,9},{9,1},{17,25},{25,17},{2,10},{10... | collective-permute-start | bytes 3145736 | tf_op jit(solution)/shard_map/ppermute | solution.py:81
  483.9 13.5 %slice-start.5 = ((s8[9437184]{0:T(1024)(128)(4,1)}), s8[4194304]{0:T(1024)(128)(4,1)S(1)}, s32[]{:S(2)}) async-start(s8[9437184]{0:T(1024)(128)(4,1)} %bitcast.415), calls=%async_computation.14 | async-start | bytes 8388608
  489.5 120.3 %collective-permute-start.34 = (bf16[8,2,32,4608]{3,2,1,0:T(8,128)(2,1)}, bf16[8,2,32,4608]{3,2,1,0:T(8,128)(2,1)}, u32[]{:S(2)}, u32[]{:S(2)}) collective-permute-start(bf16[8,2,32,4608]{3,2,1,0:T(8,128)(2,1)} %dynamic-slice_bitcast_fusion.1), channel_id=1, source_target_pairs={{0,8},{8,0},{16,24},{24,16},{1,9},{9,1},{17,25},{25,17},{2,10},{10... | collective-permute-start | bytes 14155784 | tf_op jit(solution)/shard_map/ppermute | solution.py:81
  489.6 13.9 %slice-start.8 = ((s8[4718592]{0:T(1024)(128)(4,1)}), s8[4194304]{0:T(1024)(128)(4,1)S(1)}, s32[]{:S(2)}) async-start(s8[4718592]{0:T(1024)(128)(4,1)} %bitcast.419), calls=%async_computation.17 | async-start | bytes 8388608
  513.4 18.0 %collective-permute-start.21 = (bf16[8,1,32,1024]{3,2,0,1:T(8,128)(2,1)}, bf16[8,1,32,1024]{3,2,0,1:T(8,128)(2,1)}, u32[]{:S(2)}, u32[]{:S(2)}) collective-permute-start(bf16[8,1,32,1024]{3,2,0,1:T(8,128)(2,1)} %constant_dynamic-slice_fusion.7), channel_id=1, source_target_pairs={{0,16},{8,24},{16,0},{24,8},{1,17},{9,25},{17,1},{25,9},{2,18},{10... | collective-permute-start | bytes 1572872 | tf_op jit(solution)/shard_map/ppermute | solution.py:81
  531.1 87.0 %collective-permute-start.27 = (bf16[8,2,32,4608]{3,2,0,1:T(8,128)(2,1)}, bf16[8,2,32,4608]{3,2,0,1:T(8,128)(2,1)}, u32[]{:S(2)}, u32[]{:S(2)}) collective-permute-start(bf16[8,2,32,4608]{3,2,0,1:T(8,128)(2,1)} %bitcast.354), channel_id=1, source_target_pairs={{0,8},{8,0},{16,24},{24,16},{1,9},{9,1},{17,25},{25,17},{2,10},{10... | collective-permute-start | bytes 14155784 | tf_op jit(solution)/shard_map/ppermute | solution.py:81
  532.7 8.7 collective-permute-start.22
  541.6 5.1 collective-permute-start.23
  546.8 8.0 collective-permute-start.24
  554.8 190.8 %collective-permute-start.38 = (bf16[8,2,144,1024]{3,2,1,0:T(8,128)(2,1)}, bf16[8,2,144,1024]{3,2,1,0:T(8,128)(2,1)}, u32[]{:S(2)}, u32[]{:S(2)}) collective-permute-start(bf16[8,2,144,1024]{3,2,1,0:T(8,128)(2,1)} %dynamic-slice_bitcast_fusion), channel_id=1, source_target_pairs={{0,8},{8,0},{16,24},{24,16},{1,9},{9,1},{17,25},{25,17},{2,10},{10... | collective-permute-start | bytes 14155784 | tf_op jit(solution)/shard_map/ppermute | solution.py:81
  554.8 5.5 collective-permute-start.25
  557.5 25.6 %collective-permute-start.7 = (bf16[1,1,512,1024]{3,2,1,0:T(8,128)(2,1)S(1)}, bf16[1,1,512,1024]{3,2,1,0:T(8,128)(2,1)S(1)}, u32[]{:S(2)}, u32[]{:S(2)}) collective-permute-start(bf16[1,1,512,1024]{3,2,1,0:T(8,128)(2,1)S(1)} %constant_dynamic-slice_fusion.14), channel_id=1, source_target_pairs={{0,16},{8,24},{16,0},{24,8},{1,17},{9,25},{17,1},{25,9},{2,18},{10... | collective-permute-start | bytes 3145736 | tf_op jit(solution)/shard_map/ppermute | solution.py:81
  560.3 4.6 collective-permute-start.26
  594.3 1.9 collective-permute-start.8
  596.2 5.6 collective-permute-start.9
  601.8 3.8 collective-permute-start.10
  605.6 3.7 collective-permute-start.11
  607.4 14.5 %collective-permute-start.13 = (bf16[8,2,32,2048]{3,2,0,1:T(8,128)(2,1)}, bf16[8,2,32,2048]{3,2,0,1:T(8,128)(2,1)}, u32[]{:S(2)}, u32[]{:S(2)}) collective-permute-start(bf16[8,2,32,2048]{3,2,0,1:T(8,128)(2,1)} %bitcast.355), channel_id=1, source_target_pairs={{0,8},{8,0},{16,24},{24,16},{1,9},{9,1},{17,25},{25,17},{2,10},{10... | collective-permute-start | bytes 6291464 | tf_op jit(solution)/shard_map/ppermute | solution.py:81
  609.3 22.0 %collective-permute-start.12 = (f32[2176]{0:T(1024)S(1)}, f32[2176]{0:T(1024)S(1)}, u32[]{:S(2)}, u32[]{:S(2)}) collective-permute-start(f32[2176]{0:T(1024)S(1)} %add.375), channel_id=1, source_target_pairs={{0,4},{1,5},{2,6},{3,7},{4,0},{5,1},{6,2},{7,3},{8,12},{9,13},{10,... | collective-permute-start | bytes 26120 | tf_op jit(solution)/shard_map/ppermute | solution.py:131
  616.9 79.5 %collective-permute-start.35 = (bf16[8,1,32,4608]{3,2,1,0:T(8,128)(2,1)}, bf16[8,1,32,4608]{3,2,1,0:T(8,128)(2,1)}, u32[]{:S(2)}, u32[]{:S(2)}) collective-permute-start(bf16[8,1,32,4608]{3,2,1,0:T(8,128)(2,1)} %constant_dynamic-slice_fusion.1), channel_id=1, source_target_pairs={{0,16},{8,24},{16,0},{24,8},{1,17},{9,25},{17,1},{25,9},{2,18},{10... | collective-permute-start | bytes 7077896 | tf_op jit(solution)/shard_map/ppermute | solution.py:81
  626.0 67.8 %collective-permute-start.14 = (bf16[8,1,32,2048]{3,2,0,1:T(8,128)(2,1)S(1)}, bf16[8,1,32,2048]{3,2,0,1:T(8,128)(2,1)S(1)}, u32[]{:S(2)}, u32[]{:S(2)}) collective-permute-start(bf16[8,1,32,2048]{3,2,0,1:T(8,128)(2,1)S(1)} %constant_dynamic-slice_fusion.11), channel_id=1, source_target_pairs={{0,16},{8,24},{16,0},{24,8},{1,17},{9,25},{17,1},{25,9},{2,18},{10... | collective-permute-start | bytes 3145736 | tf_op jit(solution)/shard_map/ppermute | solution.py:81
  628.4 114.2 %collective-permute-start.28 = (bf16[8,1,32,4608]{3,2,0,1:T(8,128)(2,1)}, bf16[8,1,32,4608]{3,2,0,1:T(8,128)(2,1)S(1)}, u32[]{:S(2)}, u32[]{:S(2)}) collective-permute-start(bf16[8,1,32,4608]{3,2,0,1:T(8,128)(2,1)} %constant_dynamic-slice_fusion.3), channel_id=1, source_target_pairs={{0,16},{8,24},{16,0},{24,8},{1,17},{9,25},{17,1},{25,9},{2,18},{10... | collective-permute-start | bytes 7077896 | tf_op jit(solution)/shard_map/ppermute | solution.py:81
  695.0 57.5 %collective-permute-start.15 = (bf16[1,4,32,2048]{3,2,1,0:T(8,128)(2,1)}, bf16[1,4,32,2048]{3,2,1,0:T(8,128)(2,1)}, u32[]{:S(2)}, u32[]{:S(2)}) collective-permute-start(bf16[1,4,32,2048]{3,2,1,0:T(8,128)(2,1)} %dynamic-slice_bitcast_fusion.5), channel_id=1, source_target_pairs={{0,1},{1,0},{2,3},{3,2},{4,5},{5,4},{6,7},{7,6},{8,9},{9,8},{10,11... | collective-permute-start | bytes 1572872 | tf_op jit(solution)/shard_map/ppermute | solution.py:81
  700.2 176.5 %reduce-scatter.5.cloned.1.call-start = ((), (), s32[]{:S(2)}) async-start(), calls=%async_computation.8 | async-start | bytes 2654208 | tf_op jit(solution)/shard_map/reduce_scatter | solution.py:120
  744.9 29.6 %collective-permute-start.29 = (bf16[1,4,32,4608]{3,2,1,0:T(8,128)(2,1)S(1)}, bf16[1,4,32,4608]{3,2,1,0:T(8,128)(2,1)S(1)}, u32[]{:S(2)}, u32[]{:S(2)}) collective-permute-start(bf16[1,4,32,4608]{3,2,1,0:T(8,128)(2,1)S(1)} %dynamic-slice_bitcast_fusion.3), channel_id=1, source_target_pairs={{0,1},{1,0},{2,3},{3,2},{4,5},{5,4},{6,7},{7,6},{8,9},{9,8},{10,11... | collective-permute-start | bytes 3538952 | tf_op jit(solution)/shard_map/ppermute | solution.py:81
  752.1 51.3 %collective-permute-start.39 = (bf16[8,1,144,1024]{3,2,1,0:T(8,128)(2,1)S(1)}, bf16[8,1,144,1024]{3,2,1,0:T(8,128)(2,1)S(1)}, u32[]{:S(2)}, u32[]{:S(2)}) collective-permute-start(bf16[8,1,144,1024]{3,2,1,0:T(8,128)(2,1)S(1)} %constant_dynamic-slice_fusion), channel_id=1, source_target_pairs={{0,16},{8,24},{16,0},{24,8},{1,17},{9,25},{17,1},{25,9},{2,18},{10... | collective-permute-start | bytes 7077896 | tf_op jit(solution)/shard_map/ppermute | solution.py:81
  753.7 22.4 %collective-permute-start.16 = (bf16[1,2,32,2048]{3,2,1,0:T(8,128)(2,1)S(1)}, bf16[1,2,32,2048]{3,2,1,0:T(8,128)(2,1)S(1)}, u32[]{:S(2)}, u32[]{:S(2)}) collective-permute-start(bf16[1,2,32,2048]{3,2,1,0:T(8,128)(2,1)S(1)} %dynamic-slice_bitcast_fusion.7), channel_id=1, source_target_pairs={{0,2},{1,3},{2,0},{3,1},{4,6},{5,7},{6,4},{7,5},{8,10},{9,11},{10,... | collective-permute-start | bytes 786440 | tf_op jit(solution)/shard_map/ppermute | solution.py:81
  774.9 31.0 %collective-permute-start.30 = (bf16[1,2,32,4608]{3,2,1,0:T(8,128)(2,1)S(1)}, bf16[1,2,32,4608]{3,2,1,0:T(8,128)(2,1)S(1)}, u32[]{:S(2)}, u32[]{:S(2)}) collective-permute-start(bf16[1,2,32,4608]{3,2,1,0:T(8,128)(2,1)S(1)} %dynamic-slice_bitcast_fusion.4), channel_id=1, source_target_pairs={{0,2},{1,3},{2,0},{3,1},{4,6},{5,7},{6,4},{7,5},{8,10},{9,11},{10,... | collective-permute-start | bytes 1769480 | tf_op jit(solution)/shard_map/ppermute | solution.py:81
  776.2 30.9 %collective-permute-start.17 = (bf16[1,1,32,2048]{3,2,1,0:T(8,128)(2,1)S(1)}, bf16[1,1,32,2048]{3,2,1,0:T(8,128)(2,1)S(1)}, u32[]{:S(2)}, u32[]{:S(2)}) collective-permute-start(bf16[1,1,32,2048]{3,2,1,0:T(8,128)(2,1)S(1)} %constant_dynamic-slice_fusion.10), channel_id=1, source_target_pairs={{0,4},{1,5},{2,6},{3,7},{4,0},{5,1},{6,2},{7,3},{8,12},{9,13},{10,... | collective-permute-start | bytes 393224 | tf_op jit(solution)/shard_map/ppermute | solution.py:81
  806.1 22.7 %collective-permute-start.31 = (bf16[1,1,32,4608]{3,2,1,0:T(8,128)(2,1)S(1)}, bf16[1,1,32,4608]{3,2,1,0:T(8,128)(2,1)S(1)}, u32[]{:S(2)}, u32[]{:S(2)}) collective-permute-start(bf16[1,1,32,4608]{3,2,1,0:T(8,128)(2,1)S(1)} %constant_dynamic-slice_fusion.2), channel_id=1, source_target_pairs={{0,4},{1,5},{2,6},{3,7},{4,0},{5,1},{6,2},{7,3},{8,12},{9,13},{10,... | collective-permute-start | bytes 884744 | tf_op jit(solution)/shard_map/ppermute | solution.py:81
  807.1 21.8 %collective-permute-start.18 = (bf16[1,32,2048]{2,1,0:T(8,128)(2,1)S(1)}, bf16[1,32,2048]{2,1,0:T(8,128)(2,1)S(1)}, u32[]{:S(2)}, u32[]{:S(2)}) collective-permute-start(bf16[1,32,2048]{2,1,0:T(8,128)(2,1)S(1)} %fusion.65), channel_id=1, source_target_pairs={{0,16},{8,24},{16,0},{24,8},{1,17},{9,25},{17,1},{25,9},{2,18},{10... | collective-permute-start | bytes 393224 | tf_op jit(solution)/shard_map/ppermute | solution.py:94
  828.8 6.8 collective-permute-start.32
  829.0 6.8 collective-permute-start.19
  835.7 2.1 collective-permute-start.33
  837.7 40.4 %copy-start.54 = (bf16[32,4608]{1,0:T(8,128)(2,1)S(1)}, bf16[32,4608]{1,0:T(8,128)(2,1)}, u32[]{:S(2)}) copy-start(bf16[32,4608]{1,0:T(8,128)(2,1)} %reduce-scatter.3.cloned.1.call-done) | copy-start | bytes 884740
  837.7 40.4 %collective-permute-start.36 = (bf16[1,32,4608]{2,1,0:T(8,128)(2,1)}, bf16[1,32,4608]{2,1,0:T(8,128)(2,1)S(1)}, u32[]{:S(2)}, u32[]{:S(2)}) collective-permute-start(bf16[1,32,4608]{2,1,0:T(8,128)(2,1)} %bitcast.410), channel_id=1, source_target_pairs={{0,16},{8,24},{16,0},{24,8},{1,17},{9,25},{17,1},{25,9},{2,18},{10... | collective-permute-start | bytes 884744 | tf_op jit(solution)/shard_map/ppermute | solution.py:94
  876.6 7.9 collective-permute-start.40
  878.2 6.6 collective-permute-start.37
  884.7 2.1 collective-permute-start.41
  (69 other events, 294.9 us)
Sparse Core Ops, SparseCore 0:
  10.8 54.7 all-gather.11
  68.4 50.5 all-gather.9
  122.5 73.7 all-gather.5
  199.0 57.4 all-gather.7
  259.3 80.0 all-gather.13
  700.3 70.9 reduce-scatter.2
  806.0 70.5 reduce-scatter.4
